TPU v7x, 512 devices: a whole 4x8x8 slice. The times are simulated.
512 devices in a mesh: leaf: 8 (over y), row: 64 (over z, x, core).
Axes of the slice: x: 4, y: 8, z: 8, core: 2. Of those that a mesh axis runs over, the one named last changes fastest.
Arguments:
- rhs_field: float32 [64, 262144], P(None, ('leaf', 'row')), may hold values from -6 to 6
- right_basis: float32 [3, 256, 262144], P(None, None, ('leaf', 'row')), may hold values from -6 to 6
- left_basis: float32 [3, 256, 262144], P(None, None, ('leaf', 'row')), may hold values from -0.375 to 0.375
- cores: float32 [8, 3, 512, 256], P('leaf'), as said below
Outputs:
- solution: float32 [64, 262144], P(None, ('leaf', 'row'))
Inputs may be any that keep to these rules, and one draw needn't show every extreme that they name: cores[i, k] is the same matrix for all i in one aligned block of 2**k indices; its entries have zero mean and magnitudes up to a few times 0.5 / sqrt(2 * 256 * 2**k * 32768).
All inputs are finite; a program needn't handle non-finite values.
Results may differ from a plain program's by a relative error of at most 0.0001.
Values sent between devices are 32-bit elements; how exact they have to be, the bound alone decides.
No kernel may reach another device: no remote copies, remote signals or barrier semaphores. Data moves between devices by JAX's collectives and lax.ppermute only.
A program may use at most 64 MiB of HBM per device.

v0:
```python
import jax
import jax.numpy as jnp
from jax import lax
from jax.sharding import PartitionSpec as P


def from_partner(block, axis, stride):
    count = lax.axis_size(axis)
    route = []
    for low in range(count):
        high = low | 1 << stride
        if high != low and high < count:
            route += [(low, high), (high, low)]
    return lax.ppermute(block, axis, route)


def project(field, basis):
    return lax.dot_general(
        field,
        basis,
        (((1,), (1,)), ((), ())),
        precision=lax.Precision.HIGHEST,
        preferred_element_type=jnp.float32,
    )


def node_matrix(local, level, leaf_index):
    local = lax.psum(local, "row")
    own = local
    other = local
    for bit in range(level + 1):
        received = from_partner(own, "leaf", bit)
        if bit < level:
            own = own + received
        else:
            other = received
    upper = leaf_index >> level & 1 == 1
    lower_half = jnp.where(upper, other, own)
    upper_half = jnp.where(upper, own, other)
    stacked = jnp.concatenate([lower_half, upper_half], axis=1)
    return stacked


def shards(rhs_field, right_basis, left_basis, cores):
    precise = lax.Precision.HIGHEST
    depth = right_basis.shape[0]
    leaf_index = lax.axis_index("leaf")
    field = rhs_field
    for level in range(depth):
        stacked = node_matrix(project(field, right_basis[level]), level, leaf_index)
        coeff = jnp.dot(
            stacked, cores[0, level], precision=precise, preferred_element_type=jnp.float32
        )
        field = field - jnp.dot(
            coeff, left_basis[level], precision=precise, preferred_element_type=jnp.float32
        )
    return field


def solution(mesh):
    in_specs = (
        P(None, ("leaf", "row")),
        P(None, None, ("leaf", "row")),
        P(None, None, ("leaf", "row")),
        P("leaf", None, None, None),
    )
    out_specs = P(None, ("leaf", "row"))
    return jax.shard_map(shards, mesh=mesh, in_specs=in_specs, out_specs=out_specs, check_vma=False)
```

profile of v0, /device:TPU:1, one launch (start us, length us, event | category | flops | bytes accessed | tf_op | source)
XLA Modules:
  0.0 608.9 jit_solution(2112004380187854879)
XLA Ops:
  6.5 0.0 copy-start
  6.5 0.0 copy-start.2
  6.5 0.0 all-reduce.4.cloned.1.call-start
  6.5 2.5 fusion.13
  9.0 0.0 copy-start.1
  9.0 0.0 all-reduce.4.cloned.1.call-update
  9.0 0.0 all-reduce.6.cloned.1.call-start
  9.1 187.0 %all-reduce.4.cloned.1.call-done = f32[64,256]{1,0:T(8,128)} async-done(((f32[64,256]{1,0:T(8,128)}), f32[64,256]{1,0:T(8,128)}) %all-reduce.4.cloned.1.call-update) | async-done | bytes 65552 | tf_op jit(solution)/shard_map/psum | solution.py:28
  196.1 3.1 collective-permute-start
  199.2 2.1 collective-permute-done
  201.3 0.9 broadcast_select_fusion.5
  202.2 1.4 fusion.11
  203.6 0.0 copy-done.2
  203.6 1.5 convolution_subtract_fusion.2
  205.1 0.0 copy-done
  205.1 1.2 fusion.8
  206.3 0.0 all-reduce.6.cloned.1.call-update
  206.4 0.0 all-reduce.8.cloned.1.call-start
  206.4 177.5 %all-reduce.6.cloned.1.call-done = f32[64,256]{1,0:T(8,128)} async-done(((f32[64,256]{1,0:T(8,128)}), f32[64,256]{1,0:T(8,128)}) %all-reduce.6.cloned.1.call-update) | async-done | bytes 65552 | tf_op jit(solution)/shard_map/psum | solution.py:28
  383.9 3.1 collective-permute-start.1
  387.0 2.1 collective-permute-done.1
  389.1 0.8 add.15
  389.9 4.0 collective-permute-start.2
  394.0 1.9 collective-permute-done.2
  395.9 0.0 copy-done.1
  395.9 0.4 fusion.6
  396.2 1.5 convolution_subtract_fusion.1
  397.7 1.2 fusion.3
  399.0 0.0 all-reduce.8.cloned.1.call-update
  399.0 179.3 %all-reduce.8.cloned.1.call-done = f32[64,256]{1,0:T(8,128)} async-done(((f32[64,256]{1,0:T(8,128)}), f32[64,256]{1,0:T(8,128)}) %all-reduce.8.cloned.1.call-update) | async-done | bytes 65552 | tf_op jit(solution)/shard_map/psum | solution.py:28
  578.4 3.1 collective-permute-start.3
  581.5 2.1 collective-permute-done.3
  583.6 0.8 add.16
  584.4 4.0 collective-permute-start.4
  588.5 1.9 collective-permute-done.4
  590.3 7.8 %collective-permute-start.5 = (f32[64,256]{1,0:T(8,128)S(1)}, f32[64,256]{1,0:T(8,128)S(1)}, u32[]{:S(2)}, u32[]{:S(2)}) collective-permute-start(f32[64,256]{1,0:T(8,128)S(1)} %add.17), channel_id=1, source_target_pairs={{0,256},{256,0},{64,320},{320,64},{128,384},{384,128},{192,448},{4... | collective-permute-start | bytes 196616 | tf_op jit(solution)/shard_map/ppermute | solution.py:14
  598.1 1.7 collective-permute-done.5
  599.9 0.4 fusion.1
  600.3 2.1 convolution_subtract_fusion
  (3 shorter events, 0.0 us)
Async XLA Ops:
  6.5 198.6 %copy-start = (f32[3,256,512]{2,1,0:T(8,128)S(1)}, f32[3,256,512]{2,1,0:T(8,128)}, u32[]{:S(2)}) copy-start(f32[3,256,512]{2,1,0:T(8,128)} %param.5) | copy-start | bytes 4718596
  6.5 197.1 %copy-start.2 = (f32[64,512]{1,0:T(8,128)S(1)}, f32[64,512]{1,0:T(8,128)}, u32[]{:S(2)}) copy-start(f32[64,512]{1,0:T(8,128)} %param.4) | copy-start | bytes 393220
  6.5 189.6 %all-reduce.4.cloned.1.call-start = ((), (), s32[]{:S(2)}) async-start(), calls=%async_computation | async-start | bytes 131072 | tf_op jit(solution)/shard_map/psum | solution.py:28
  9.0 386.8 %copy-start.1 = (f32[1,3,512,256]{3,2,1,0:T(8,128)S(1)}, f32[1,3,512,256]{3,2,1,0:T(8,128)}, u32[]{:S(2)}) copy-start(f32[1,3,512,256]{3,2,1,0:T(8,128)} %param.7) | copy-start | bytes 4718596
  9.0 374.8 %all-reduce.6.cloned.1.call-start = ((), (), s32[]{:S(2)}) async-start(), calls=%async_computation.1 | async-start | bytes 131072 | tf_op jit(solution)/shard_map/psum | solution.py:28
  196.1 5.2 collective-permute-start
  206.4 372.0 %all-reduce.8.cloned.1.call-start = ((), (), s32[]{:S(2)}) async-start(), calls=%async_computation.2 | async-start | bytes 131072 | tf_op jit(solution)/shard_map/psum | solution.py:28
  383.9 5.2 collective-permute-start.1
  389.9 5.9 collective-permute-start.2
  578.4 5.2 collective-permute-start.3
  584.4 5.9 collective-permute-start.4
  590.3 9.5 %collective-permute-start.5 = (f32[64,256]{1,0:T(8,128)S(1)}, f32[64,256]{1,0:T(8,128)S(1)}, u32[]{:S(2)}, u32[]{:S(2)}) collective-permute-start(f32[64,256]{1,0:T(8,128)S(1)} %add.17), channel_id=1, source_target_pairs={{0,256},{256,0},{64,320},{320,64},{128,384},{384,128},{192,448},{4... | collective-permute-start | bytes 196616 | tf_op jit(solution)/shard_map/ppermute | solution.py:14
Sparse Core Ops, SparseCore 0:
  10.8 185.2 all-reduce.3
  206.5 177.3 all-reduce.5
  399.1 179.1 all-reduce.7
where the time goes:
time: 613 us; the launch traced here: 609 us
  waiting for transfers between devices  556 us (91%)
  starting transfers between devices  25.3 us (4%)
  between operations  13.2 us (2%)
  matrix products  12.2 us (2%)
    psum x3, waiting for transfers between devices, node_matrix(): local = lax.psum(local, 'row')  544 us
    ppermute x6, starting transfers between devices, from_partner(): return lax.ppermute(block, axis, route)  25.2 us
  transfers between devices with their start and end apart: 9, of which 9 were waited for; matrix products, arithmetic and copies ran while one was open for 0% of the time, Pallas kernels for 0%

commit v1 on v0

v1 whole, which is shorter than its diff:
```python
import jax
import jax.numpy as jnp
from jax import lax
from jax.experimental import pallas as pl
from jax.experimental.pallas import tpu as pltpu
from jax.sharding import Mesh, PartitionSpec as P

LEAF = ("y2", "y1", "y0")
HALF = 16
LANES = 128


def mul(a, b):
    return lax.dot_general(
        a,
        b,
        (((1,), (0,)), ((), ())),
        precision=lax.Precision.HIGHEST,
        preferred_element_type=jnp.float32,
    )


def mul_t(a, b):
    return lax.dot_general(
        a,
        b,
        (((1,), (1,)), ((), ())),
        precision=lax.Precision.HIGHEST,
        preferred_element_type=jnp.float32,
    )


def gram_kernel(field_ref, right_ref, left_ref, out_ref):
    field = field_ref[...]
    peers = out_ref.shape[0]

    def put_packed(block, row, value):
        for s in range(peers):
            top = value[HALF * s : HALF * (s + 1)]
            low = value[LANES + HALF * s : LANES + HALF * (s + 1)]
            out_ref[s, block, row : row + HALF, :] = jnp.concatenate([top, low], axis=1)

    def put(block, value):
        for s in range(peers):
            for h in range(2):
                out_ref[s, block, HALF * h : HALF * (h + 1), :] = value[
                    LANES * h + HALF * s : LANES * h + HALF * (s + 1)
                ]

    put_packed(0, 0, mul_t(right_ref[0], field))
    put_packed(0, HALF, mul_t(right_ref[1], field))
    put_packed(1, 0, mul_t(right_ref[2], field))
    for s in range(peers):
        out_ref[s, 1, HALF:, :] = jnp.zeros((HALF, LANES), jnp.float32)
    block = 2
    for j, k in ((0, 1), (0, 2), (1, 2)):
        gram = mul_t(right_ref[k], left_ref[j])
        put(block, gram[:, :LANES])
        put(block + 1, gram[:, LANES:])
        block += 2


def sum_kernel(in_ref, out_ref):
    total = in_ref[0]
    for s in range(1, in_ref.shape[0]):
        total = total + in_ref[s]
    out_ref[...] = total


def sum_spread_kernel(in_ref, out_ref):
    total = in_ref[0]
    for s in range(1, in_ref.shape[0]):
        total = total + in_ref[s]
    for s in range(out_ref.shape[0]):
        out_ref[s] = total


def coefficients(got_ref, core_ref):
    sides = []
    group = got_ref.shape[0] // 2
    for side in range(2):
        part = got_ref[side * group]
        for g in range(1, group):
            part = part + got_ref[side * group + g]
        turned = part.reshape(LANES, LANES).T
        sides += [turned[: LANES // 2], turned[LANES // 2 :]]
    stacked = jnp.concatenate(sides, axis=1)
    return mul(stacked, core_ref[0, 0])


def packed(value):
    return jnp.concatenate([value[:HALF], value[HALF:]], axis=1)


def gram_block(blocks_ref, first):
    return jnp.concatenate([blocks_ref[first], blocks_ref[first + 1]], axis=1)


def level0_kernel(got_ref, core_ref, blocks_ref, coeff_ref, out_ref):
    coeff = coefficients(got_ref, core_ref)
    coeff_ref[...] = coeff
    fresh = blocks_ref[0, HALF:, :] - packed(mul_t(gram_block(blocks_ref, 2), coeff))
    for s in range(out_ref.shape[0]):
        out_ref[s] = fresh


def level1_kernel(got_ref, core_ref, blocks_ref, coeff0_ref, coeff_ref, out_ref):
    coeff = coefficients(got_ref, core_ref)
    coeff_ref[...] = coeff
    change = mul_t(gram_block(blocks_ref, 4), coeff0_ref[...])
    change = change + mul_t(gram_block(blocks_ref, 6), coeff)
    fresh = blocks_ref[1, :HALF, :] - packed(change)
    for s in range(out_ref.shape[0]):
        out_ref[s] = fresh


def level2_kernel(got_ref, core_ref, coeff0_ref, coeff1_ref, field_ref, left_ref, out_ref):
    change = mul(coeff0_ref[...], left_ref[0]) + mul(coeff1_ref[...], left_ref[1])
    coeff = coefficients(got_ref, core_ref)
    change = change + mul(coeff, left_ref[2])
    out_ref[...] = field_ref[...] - change


def whole(x):
    return pl.BlockSpec(x.shape, lambda i: (0,) * x.ndim)


def core_of(cores, level):
    return pl.BlockSpec((1, 1) + cores.shape[2:], lambda i: (0, level, 0, 0))


def call(kernel, out_shape, args, in_specs=None):
    if in_specs is None:
        in_specs = [whole(x) for x in args]
    single = not isinstance(out_shape[0], tuple)
    shapes = (out_shape,) if single else out_shape
    out = tuple(jax.ShapeDtypeStruct(s, jnp.float32) for s in shapes)
    specs = tuple(whole(o) for o in out)
    return pl.pallas_call(
        kernel,
        grid=(1,),
        out_shape=out[0] if single else out,
        in_specs=in_specs,
        out_specs=specs[0] if single else specs,
        compiler_params=pltpu.CompilerParams(vmem_limit_bytes=32 << 20),
    )(*args)


def swap(x, axes):
    return lax.all_to_all(x, axes, 0, 0, tiled=True)


def shards(rhs_field, right_basis, left_basis, cores):
    nz, ns = lax.axis_size("z"), lax.axis_size("xc")
    tile = (2 * HALF, LANES)
    half = (HALF, LANES)
    rhs, rank = rhs_field.shape[0], right_basis.shape[1]

    part = call(gram_kernel, (ns, nz) + tile, (rhs_field, right_basis, left_basis))
    part = swap(part, "xc")
    part = call(sum_kernel, (nz,) + tile, (part,))
    part = swap(part, "z")
    part = call(sum_spread_kernel, (nz,) + tile, (part,))
    blocks = swap(part, "z")

    send = jnp.broadcast_to(blocks[0, :HALF], (2 * ns,) + half)
    got = swap(send, ("y0", "xc")).reshape((2, ns) + half)
    coeff0, send = call(
        level0_kernel,
        ((rhs, rank), (4 * ns,) + half),
        (got, cores, blocks),
        [whole(got), core_of(cores, 0), whole(blocks)],
    )
    got = swap(send, ("y1", "y0", "xc")).reshape((4, ns) + half)
    coeff1, send = call(
        level1_kernel,
        ((rhs, rank), (8 * ns,) + half),
        (got, cores, blocks, coeff0),
        [whole(got), core_of(cores, 1), whole(blocks), whole(coeff0)],
    )
    got = swap(send, ("y2", "y1", "y0", "xc")).reshape((8, ns) + half)
    return call(
        level2_kernel,
        rhs_field.shape,
        (got, cores, coeff0, coeff1, rhs_field, left_basis),
        [whole(got), core_of(cores, 2), whole(coeff0), whole(coeff1), whole(rhs_field), whole(left_basis)],
    )


def solution(mesh):
    ns = 8
    devices = mesh.devices.reshape((2, 2, 2, mesh.shape["row"] // ns, ns))
    fine = Mesh(devices, LEAF + ("z", "xc"))
    points = LEAF + ("z", "xc")
    in_specs = (
        P(None, points),
        P(None, None, points),
        P(None, None, points),
        P(LEAF, None, None, None),
    )
    return jax.shard_map(shards, mesh=fine, in_specs=in_specs, out_specs=P(None, points), check_vma=False)
```

time: 613 us -> 112 us (0.18)
  waiting for transfers between devices: 556 us -> 0 us
  blocking collectives: 0 us -> 102 us
  starting transfers between devices: 25.3 us -> 0 us
  between operations: 13.2 us -> 0.04 us
  matrix products: 12.2 us -> 0 us
  Pallas kernels: 0 us -> 6.39 us
    psum x3 -> x0, waiting for transfers between devices: 544 us -> none  [node_matrix(): local = lax.psum(local, 'row')]
    all_to_all x0 -> x6, blocking collectives: none -> 102 us  [swap(): return lax.all_to_all(x, axes, 0, 0, tiled=True)]
    ppermute x6 -> x0, starting transfers between devices: 25.2 us -> none  [from_partner(): return lax.ppermute(block, axis, route)]
    dot_general x9 -> x0, matrix products: 12.2 us -> none  [the longest x3 5.1 us: shards(): jnp.dot(coeff, left_basis[level], precision=precise, preferred_element_ty...]
    ppermute x6 -> x0, waiting for transfers between devices: 11.8 us -> none  [from_partner(): return lax.ppermute(block, axis, route)]
    pallas_call x0 -> x6, Pallas kernels: none -> 6.39 us  [call(): pl.pallas_call(kernel, grid=(1,), out_shape=out[0] if single else out, in...]
  transfers between devices with their start and end apart: 9 -> 0, of which waited for: 9 -> 0; matrix products, arithmetic and copies ran while one was open for 0% -> 0% of each run, Pallas kernels for 0% -> 0%
where the time goes in v1:
time: 112 us
  blocking collectives  102 us (91%)
  Pallas kernels  6.39 us (6%)
  local copies, waits for them, and re-layouts  3.74 us (3%)
    all_to_all x6, blocking collectives, swap(): return lax.all_to_all(x, axes, 0, 0, tiled=True)  102 us
    pallas_call x6, Pallas kernels, call(): pl.pallas_call(kernel, grid=(1,), out_shape=out[0] if single else out, in...  6.39 us
    unnamed x12, local copies, waits for them, and re-layouts  3.73 us

profile of v1, /device:TPU:1, one launch (start us, length us, event | category | flops | bytes accessed | tf_op | source)
XLA Modules:
  0.0 111.9 jit_solution(4346531111985740230)
XLA Ops:
  0.0 0.0 copy-start.1
  0.0 1.4 %copy-done.1 = f32[3,256,512]{2,1,0:T(8,128)S(1)} copy-done((f32[3,256,512]{2,1,0:T(8,128)S(1)}, f32[3,256,512]{2,1,0:T(8,128)}, u32[]{:S(2)}) %copy-start.1) | copy-done | bytes 1572888
  1.4 0.0 copy-start.3
  1.4 1.4 %copy-done.3 = f32[3,256,512]{2,1,0:T(8,128)S(1)} copy-done((f32[3,256,512]{2,1,0:T(8,128)S(1)}, f32[3,256,512]{2,1,0:T(8,128)}, u32[]{:S(2)}) %copy-start.3) | copy-done | bytes 1572888
  2.8 0.0 copy-start.4
  2.8 0.9 copy-done.4
  3.7 2.7 %shard_map.46 = f32[8,8,32,128]{3,2,1,0:T(8,128)S(1)} custom-call(f32[64,512]{1,0:T(8,128)S(1)} %copy-done.4, f32[3,256,512]{2,1,0:T(8,128)S(1)} %copy-done.3, f32[3,256,512]{2,1,0:T(8,128)S(1)} %copy-done.1), custom_call_target="tpu_custom_call" | custom-call | tf_op jit(solution)/shard_map/pallas_call | solution.py:139
  6.4 24.4 %all_to_all.30.in_ref = f32[8,8,32,128]{3,2,1,0:T(8,128)S(1)} all-to-all(f32[8,8,32,128]{3,2,1,0:T(8,128)S(1)} %shard_map.46), channel_id=1, replica_groups=mesh['y2'=2,'y1'=2,'y0'=2,'z'=8,'xc'=8] {'xc'}, dimensions={0} | all-to-all | bytes 2097152 | tf_op jit(solution)/shard_map/all_to_all | solution.py:150
  30.8 0.0 copy-start
  30.8 0.1 shard_map.47
  30.8 14.3 %all_to_all.31.in_ref = f32[8,32,128]{2,1,0:T(8,128)S(1)} all-to-all(f32[8,32,128]{2,1,0:T(8,128)S(1)} %shard_map.47), channel_id=1, replica_groups=mesh['y2'=2,'y1'=2,'y0'=2,'z'=8,'xc'=8] {'z'}, dimensions={0} | all-to-all | bytes 262144 | tf_op jit(solution)/shard_map/all_to_all | solution.py:150
  45.2 10.4 %all_to_all.32.blocks_ref = f32[8,32,128]{2,1,0:T(8,128)S(1)} all-to-all(f32[8,32,128]{2,1,0:T(8,128)S(1)} %shard_map.48), channel_id=1, replica_groups=mesh['y2'=2,'y1'=2,'y0'=2,'z'=8,'xc'=8] {'z'}, dimensions={0} | all-to-all | bytes 262144 | tf_op jit(solution)/shard_map/all_to_all | solution.py:150
  55.6 12.8 %all_to_all.33 = f32[16,16,128]{2,1,0:T(8,128)S(1)} all-to-all(f32[16,16,128]{2,1,0:T(8,128)S(1)} %broadcast_in_dim.3), channel_id=1, replica_groups=mesh['y2'=2,'y1'=2,'y0'=2,'z'=8,'xc'=8] {'y0','xc'}, dimensions={0} | all-to-all | bytes 262144 | tf_op jit(solution)/shard_map/all_to_all | solution.py:150
  68.4 0.0 copy-done
  68.4 0.8 shard_map.49
  69.2 16.1 %all_to_all.34 = f32[32,16,128]{2,1,0:T(8,128)S(1)} all-to-all(f32[32,16,128]{2,1,0:T(8,128)S(1)} %get-tuple-element.9), channel_id=1, replica_groups=mesh['y2'=2,'y1'=2,'y0'=2,'z'=8,'xc'=8] {'y1','y0','xc'}, dimensions={0} | all-to-all | bytes 524288 | tf_op jit(solution)/shard_map/all_to_all | solution.py:150
  85.2 0.0 copy-start.2
  85.2 0.0 copy-start.5
  85.2 0.9 shard_map.50
  86.2 23.8 %all_to_all.35 = f32[64,16,128]{2,1,0:T(8,128)S(1)} all-to-all(f32[64,16,128]{2,1,0:T(8,128)S(1)} %get-tuple-element.11), channel_id=1, replica_groups=mesh['y2'=2,'y1'=2,'y0'=2,'z'=8,'xc'=8] {'y2','y1','y0','xc'}, dimensions={0} | all-to-all | bytes 1048576 | tf_op jit(solution)/shard_map/all_to_all | solution.py:150
  110.0 0.0 copy-done.2
  110.0 0.0 copy-done.5
  110.0 1.9 %shard_map.51 = f32[64,512]{1,0:T(8,128)} custom-call(f32[8,8,16,128]{3,2,1,0:T(8,128)S(1)} %bitcast.5, f32[1,3,512,256]{3,2,1,0:T(8,128)S(1)} %copy-done, f32[64,256]{1,0:T(8,128)S(1)} %get-tuple-element.10.coeff0_ref, f32[64,256]{1,0:T(8,128)S(1)} %get-tuple-element.12.coeff1_ref, f32[64,512]{1,0:T(8,128)S(1)} %copy-done.5, f32[3,256,512]{2,1,0:T(8,128)S(1)} %copy-done.2), custom_call_target="tpu_custom_call" | custom-call | tf_op jit(solution)/shard_map/pallas_call | solution.py:139
  (3 shorter events, 0.0 us)
Async XLA Ops:
  0.0 1.4 %copy-start.1 = (f32[3,256,512]{2,1,0:T(8,128)S(1)}, f32[3,256,512]{2,1,0:T(8,128)}, u32[]{:S(2)}) copy-start(f32[3,256,512]{2,1,0:T(8,128)} %left_ref.3) | copy-start | bytes 4718596
  1.4 1.4 %copy-start.3 = (f32[3,256,512]{2,1,0:T(8,128)S(1)}, f32[3,256,512]{2,1,0:T(8,128)}, u32[]{:S(2)}) copy-start(f32[3,256,512]{2,1,0:T(8,128)} %right_ref.1) | copy-start | bytes 4718596
  2.8 0.9 copy-start.4
  30.8 37.6 %copy-start = (f32[1,3,512,256]{3,2,1,0:T(8,128)S(1)}, f32[1,3,512,256]{3,2,1,0:T(8,128)}, u32[]{:S(2)}) copy-start(f32[1,3,512,256]{3,2,1,0:T(8,128)} %core_ref.5) | copy-start | bytes 4718596
  85.2 24.8 %copy-start.2 = (f32[3,256,512]{2,1,0:T(8,128)S(1)}, f32[3,256,512]{2,1,0:T(8,128)}, u32[]{:S(2)}) copy-start(f32[3,256,512]{2,1,0:T(8,128)} %left_ref.3) | copy-start | bytes 4718596
  85.2 24.8 %copy-start.5 = (f32[64,512]{1,0:T(8,128)S(1)}, f32[64,512]{1,0:T(8,128)}, u32[]{:S(2)}) copy-start(f32[64,512]{1,0:T(8,128)} %field_ref.3) | copy-start | bytes 393220

commit v2 on v1

v2 whole, which is shorter than its diff:
```python
import functools

import jax
import jax.numpy as jnp
from jax import lax
from jax.experimental import pallas as pl
from jax.experimental.pallas import tpu as pltpu
from jax.sharding import Mesh, PartitionSpec as P

LEAF = ("y2", "y1", "y0")
CHIP = ("c", "x")
HALF = 16
LANES = 128
BLOCKS = 8


def halves(a):
    high = a.astype(jnp.bfloat16)
    return high, (a - high.astype(jnp.float32)).astype(jnp.bfloat16)


def product(a, b, dims):
    def one(u, v):
        return lax.dot_general(u, v, (dims, ((), ())), preferred_element_type=jnp.float32)

    return one(a[0], b[0]) + (one(a[0], b[1]) + one(a[1], b[0]))


def mul(a, b):
    return product(halves(a), halves(b), ((1,), (0,)))


def mul_t(a, b):
    return product(halves(a), halves(b), ((1,), (1,)))


def gram_kernel(own, field_hbm, right_hbm, left_hbm, out_ref, field, right, left, sems):
    core = lax.axis_index("c")
    side = core if own else 1 - core
    depth, _, rows = right.shape[:3]
    copies = []

    def fetch(src, dst):
        copy = pltpu.make_async_copy(src, dst, sems.at[len(copies)])
        copy.start()
        copies.append(copy)
        return copy

    got_field = fetch(field_hbm, field)
    got_right = [
        [fetch(right_hbm.at[k, pl.ds(2 * rows * h + rows * side, rows), :], right.at[k, h]) for h in range(2)]
        for k in range(depth)
    ]
    got_left = [fetch(left_hbm.at[j], left.at[j]) for j in range(left.shape[0])]
    peers = out_ref.shape[0]

    def put_packed(block, row, value):
        for s in range(peers):
            top = value[HALF * s : HALF * (s + 1)]
            low = value[rows + HALF * s : rows + HALF * (s + 1)]
            out_ref[s, block, row : row + HALF, :] = jnp.concatenate([top, low], axis=1)

    def put(block, value):
        for s in range(peers):
            for h in range(2):
                out_ref[s, block, HALF * h : HALF * (h + 1), :] = value[
                    rows * h + HALF * s : rows * h + HALF * (s + 1)
                ]

    for s in range(peers):
        out_ref[s, 1, HALF:, :] = jnp.zeros((HALF, LANES), jnp.float32)
    got_field.wait()
    rhs = halves(field[...])
    mine = []
    for k in range(depth):
        for h in range(2):
            got_right[k][h].wait()
        mine.append(halves(right[k].reshape(2 * rows, right.shape[3])))
        put_packed(k // 2, HALF * (k % 2), product(mine[k], rhs, ((1,), (1,))))
    for j in range(left.shape[0]):
        got_left[j].wait()
        other = halves(left[j])
        for k in range(j + 1, depth):
            gram = product(mine[k], other, ((1,), (1,)))
            block = 2 * (j + k)
            put(block, gram[:, :LANES])
            put(block + 1, gram[:, LANES:])


def gram_rows(own, field, right, left):
    depth, rank, points = right.shape
    rows = rank // 4
    scratch = [
        pltpu.VMEM(field.shape, jnp.float32),
        pltpu.VMEM((depth, 2, rows, points), jnp.float32),
        pltpu.VMEM((depth - 1, rank, points), jnp.float32),
        pltpu.SemaphoreType.DMA((1 + 2 * depth + depth - 1,)),
    ]
    return pl.pallas_call(
        functools.partial(gram_kernel, own),
        out_shape=jax.ShapeDtypeStruct((rows // HALF, BLOCKS, 2 * HALF, LANES), jnp.float32),
        in_specs=[pl.BlockSpec(memory_space=pltpu.HBM)] * 3,
        out_specs=pl.BlockSpec(memory_space=pltpu.VMEM),
        scratch_shapes=scratch,
        cost_estimate=pl.CostEstimate(flops=800_000_000, bytes_accessed=2_500_000, transcendentals=0),
        compiler_params=pltpu.CompilerParams(vmem_limit_bytes=54000 << 10),
    )(field, right, left)


def add_kernel(a_ref, b_ref, out_ref):
    out_ref[...] = a_ref[...] + b_ref[...]


def sum_kernel(in_ref, out_ref):
    total = in_ref[0]
    for s in range(1, in_ref.shape[0]):
        total = total + in_ref[s]
    out_ref[...] = total


def sum_spread_kernel(in_ref, out_ref):
    total = in_ref[0]
    for s in range(1, in_ref.shape[0]):
        total = total + in_ref[s]
    for s in range(out_ref.shape[0]):
        out_ref[s] = total


def coefficients(parts, core_ref):
    sides = []
    for part in parts:
        turned = part.reshape(LANES, LANES).T
        sides += [turned[: LANES // 2], turned[LANES // 2 :]]
    return mul(jnp.concatenate(sides, axis=1), core_ref[0, 0])


def two_sides(got_ref):
    group = got_ref.shape[0] // 2
    parts = []
    for side in range(2):
        part = got_ref[side * group]
        for g in range(1, group):
            part = part + got_ref[side * group + g]
        parts.append(part)
    return parts


def quads_kernel(got_ref, out_ref):
    for side, part in enumerate(two_sides(got_ref)):
        for s in range(out_ref.shape[0]):
            out_ref[s, side] = part


def packed(value):
    return jnp.concatenate([value[:HALF], value[HALF:]], axis=1)


def gram_block(blocks_ref, first):
    return jnp.concatenate([blocks_ref[first], blocks_ref[first + 1]], axis=1)


def level0_kernel(got_ref, core_ref, blocks_ref, coeff_ref, out_ref):
    coeff = coefficients(two_sides(got_ref), core_ref)
    coeff_ref[...] = coeff
    fresh = blocks_ref[0, HALF:, :] - packed(mul_t(gram_block(blocks_ref, 2), coeff))
    for s in range(out_ref.shape[0]):
        out_ref[s] = fresh


def level1_kernel(got_ref, core_ref, blocks_ref, coeff0_ref, coeff_ref, out_ref):
    coeff = coefficients(two_sides(got_ref), core_ref)
    coeff_ref[...] = coeff
    change = mul_t(gram_block(blocks_ref, 4), coeff0_ref[...])
    change = change + mul_t(gram_block(blocks_ref, 6), coeff)
    fresh = blocks_ref[1, :HALF, :] - packed(change)
    for s in range(out_ref.shape[0]):
        out_ref[s] = fresh


def level2_kernel(got_ref, core_ref, coeff0_ref, coeff1_ref, field_ref, left_ref, out_ref):
    change = mul(coeff0_ref[...], left_ref[0]) + mul(coeff1_ref[...], left_ref[1])
    coeff = coefficients([got_ref[:, 0], got_ref[:, 1]], core_ref)
    change = change + mul(coeff, left_ref[2])
    out_ref[...] = field_ref[...] - change


def whole(x):
    return pl.BlockSpec(x.shape, lambda i: (0,) * x.ndim)


def core_of(cores, level):
    return pl.BlockSpec((1, 1) + cores.shape[2:], lambda i: (0, level, 0, 0))


def call(kernel, out_shape, args, in_specs=None):
    if in_specs is None:
        in_specs = [whole(x) for x in args]
    single = not isinstance(out_shape[0], tuple)
    shapes = (out_shape,) if single else out_shape
    out = tuple(jax.ShapeDtypeStruct(s, jnp.float32) for s in shapes)
    specs = tuple(whole(o) for o in out)
    return pl.pallas_call(
        kernel,
        grid=(1,),
        out_shape=out[0] if single else out,
        in_specs=in_specs,
        out_specs=specs[0] if single else specs,
        compiler_params=pltpu.CompilerParams(vmem_limit_bytes=32 << 20),
    )(*args)


def swap(x, axes):
    return lax.all_to_all(x, axes, 0, 0, tiled=True)


def shards(rhs_field, right_basis, left_basis, cores):
    nz, nx = lax.axis_size("z"), lax.axis_size("x")
    ns = 2 * nx
    tile = (2 * HALF, LANES)
    half = (HALF, LANES)
    rhs, rank = rhs_field.shape[0], right_basis.shape[1]

    theirs = gram_rows(False, rhs_field, right_basis, left_basis)
    theirs = lax.ppermute(theirs, "c", [(0, 1), (1, 0)])
    mine = gram_rows(True, rhs_field, right_basis, left_basis)
    part = call(add_kernel, mine.shape, (mine, theirs))
    part = swap(part, "x")
    part = call(sum_kernel, (nz,) + tile, (part,))
    part = swap(part, "z")
    part = call(sum_spread_kernel, (nz,) + tile, (part,))
    blocks = swap(part, "z")

    send = jnp.broadcast_to(blocks[0, :HALF], (2 * ns,) + half)
    got = swap(send, ("y0",) + CHIP).reshape((2, ns) + half)
    coeff0, send = call(
        level0_kernel,
        ((rhs, rank), (4 * ns,) + half),
        (got, cores, blocks),
        [whole(got), core_of(cores, 0), whole(blocks)],
    )
    got = swap(send, ("y1", "y0") + CHIP).reshape((4, ns) + half)
    coeff1, send = call(
        level1_kernel,
        ((rhs, rank), (8,) + half),
        (got, cores, blocks, coeff0),
        [whole(got), core_of(cores, 1), whole(blocks), whole(coeff0)],
    )
    got = swap(send, LEAF)
    send = call(quads_kernel, (ns, 2) + half, (got,))
    got = swap(send, CHIP)
    return call(
        level2_kernel,
        rhs_field.shape,
        (got, cores, coeff0, coeff1, rhs_field, left_basis),
        [whole(got), core_of(cores, 2), whole(coeff0), whole(coeff1), whole(rhs_field), whole(left_basis)],
    )


def solution(mesh):
    nx, cores_of_chip = 4, 2
    nz = mesh.shape["row"] // (nx * cores_of_chip)
    points = LEAF + ("z", "x", "c")
    fine = Mesh(mesh.devices.reshape((2, 2, 2, nz, nx, cores_of_chip)), points)
    in_specs = (
        P(None, points),
        P(None, None, points),
        P(None, None, points),
        P(LEAF, None, None, None),
    )
    return jax.shard_map(shards, mesh=fine, in_specs=in_specs, out_specs=P(None, points), check_vma=False)
```

time: 112 us -> 107 us (0.955)
  blocking collectives: 102 us -> 86.4 us
  starting transfers between devices: 0 us -> 8.79 us
  Pallas kernels: 6.39 us -> 9.94 us
  local copies, waits for them, and re-layouts: 3.74 us -> 0.93 us
    all_to_all x6 -> x7, blocking collectives: 102 us -> 86.4 us  [swap(): return lax.all_to_all(x, axes, 0, 0, tiled=True)]
    ppermute x0 -> x1, starting transfers between devices: none -> 8.79 us  [shards(): theirs = lax.ppermute(theirs, 'c', [(0, 1), (1, 0)])]
    pallas_call x0 -> x2, Pallas kernels: none -> 7.31 us  [gram_rows(): pl.pallas_call(functools.partial(gram_kernel, own), out_shape=jax.ShapeDt...]
    pallas_call x6 -> x7, Pallas kernels: 6.39 us -> 2.64 us  [call(): pl.pallas_call(kernel, grid=(1,), out_shape=out[0] if single else out, in...]
    unnamed x12 -> x6, local copies, waits for them, and re-layouts: 3.73 us -> 0.92 us
  transfers between devices with their start and end apart: 0 -> 1, of which waited for: 0 -> 0; matrix products, arithmetic and copies ran while one was open for 0% -> 0% of each run, Pallas kernels for 0% -> 3%
where the time goes in v2:
time: 107 us; the launch traced here: 106 us
  blocking collectives  86.4 us (81%)
  Pallas kernels  9.94 us (9%)
  starting transfers between devices  8.79 us (8%)
    all_to_all x7, blocking collectives, swap(): return lax.all_to_all(x, axes, 0, 0, tiled=True)  86.4 us
    ppermute x1, starting transfers between devices, shards(): theirs = lax.ppermute(theirs, 'c', [(0, 1), (1, 0)])  8.79 us
    pallas_call x2, Pallas kernels, gram_rows(): pl.pallas_call(functools.partial(gram_kernel, own), out_shape=jax.ShapeDt...  7.31 us
    pallas_call x7, Pallas kernels, call(): pl.pallas_call(kernel, grid=(1,), out_shape=out[0] if single else out, in...  2.64 us
  transfers between devices with their start and end apart: 1, of which 0 were waited for; matrix products, arithmetic and copies ran while one was open for 0% of the time, Pallas kernels for 3%

profile of v2, /device:TPU:1, one launch (start us, length us, event | category | flops | bytes accessed | tf_op | source)
XLA Modules:
  0.0 106.1 jit_solution(11443524382062438927)
XLA Ops:
  0.0 0.0 copy-start.2
  0.0 0.9 copy-done.2
  0.9 3.6 %shard_map.47 = f32[4,8,32,128]{3,2,1,0:T(8,128)S(1)} custom-call(f32[64,512]{1,0:T(8,128)S(1)} %copy-done.2, f32[3,256,512]{2,1,0:T(8,128)} %right_hbm.3, f32[3,256,512]{2,1,0:T(8,128)} %left_ref.1), custom_call_target="tpu_custom_call" | custom-call | flops 800000000 | bytes 2500000 | tf_op jit(solution)/shard_map/pallas_call | solution.py:99
  4.5 8.8 %collective-permute-start = (f32[4,8,32,128]{3,2,1,0:T(8,128)S(1)}, f32[4,8,32,128]{3,2,1,0:T(8,128)S(1)}, u32[]{:S(2)}, u32[]{:S(2)}) collective-permute-start(f32[4,8,32,128]{3,2,1,0:T(8,128)S(1)} %shard_map.47), channel_id=1, source_target_pairs={{0,1},{1,0},{2,3},{3,2},{4,5},{5,4},{6,7},{7,6},{8,9},{9,8},{10,11... | collective-permute-start | bytes 1572872 | tf_op jit(solution)/shard_map/ppermute | solution.py:224
  13.3 3.7 %shard_map.46.a_ref = f32[4,8,32,128]{3,2,1,0:T(8,128)S(1)} custom-call(f32[64,512]{1,0:T(8,128)S(1)} %copy-done.2, f32[3,256,512]{2,1,0:T(8,128)} %right_hbm.3, f32[3,256,512]{2,1,0:T(8,128)} %left_ref.1), custom_call_target="tpu_custom_call" | custom-call | flops 800000000 | bytes 2500000 | tf_op jit(solution)/shard_map/pallas_call | solution.py:99
  17.0 0.0 collective-permute-done.b_ref
  17.0 0.1 shard_map.48
  17.1 0.0 copy-start.1
  17.1 11.9 %all_to_all.35.in_ref = f32[4,8,32,128]{3,2,1,0:T(8,128)S(1)} all-to-all(f32[4,8,32,128]{3,2,1,0:T(8,128)S(1)} %shard_map.48), channel_id=1, replica_groups=mesh['y2'=2,'y1'=2,'y0'=2,'z'=8,'x'=4,'c'=2] {'x'}, dimensions={0} | all-to-all | bytes 1048576 | tf_op jit(solution)/shard_map/all_to_all | solution.py:213
  29.0 13.9 %all_to_all.36.in_ref = f32[8,32,128]{2,1,0:T(8,128)S(1)} all-to-all(f32[8,32,128]{2,1,0:T(8,128)S(1)} %shard_map.49), channel_id=1, replica_groups=mesh['y2'=2,'y1'=2,'y0'=2,'z'=8,'x'=4,'c'=2] {'z'}, dimensions={0} | all-to-all | bytes 262144 | tf_op jit(solution)/shard_map/all_to_all | solution.py:213
  42.9 10.4 %all_to_all.37.blocks_ref = f32[8,32,128]{2,1,0:T(8,128)S(1)} all-to-all(f32[8,32,128]{2,1,0:T(8,128)S(1)} %shard_map.50), channel_id=1, replica_groups=mesh['y2'=2,'y1'=2,'y0'=2,'z'=8,'x'=4,'c'=2] {'z'}, dimensions={0} | all-to-all | bytes 262144 | tf_op jit(solution)/shard_map/all_to_all | solution.py:213
  53.4 12.9 %all_to_all.38 = f32[16,16,128]{2,1,0:T(8,128)S(1)} all-to-all(f32[16,16,128]{2,1,0:T(8,128)S(1)} %broadcast_in_dim.3), channel_id=1, replica_groups=mesh['y2'=2,'y1'=2,'y0'=2,'z'=8,'x'=4,'c'=2] {'y0','c','x'}, dimensions={0} | all-to-all | bytes 262144 | tf_op jit(solution)/shard_map/all_to_all | solution.py:213
  66.3 0.0 copy-done.1
  66.3 0.6 shard_map.51
  66.9 0.0 copy-start
  66.9 16.5 %all_to_all.39 = f32[32,16,128]{2,1,0:T(8,128)S(1)} all-to-all(f32[32,16,128]{2,1,0:T(8,128)S(1)} %get-tuple-element.9), channel_id=1, replica_groups=mesh['y2'=2,'y1'=2,'y0'=2,'z'=8,'x'=4,'c'=2] {'y1','y0','c','x'}, dimensions={0} | all-to-all | bytes 524288 | tf_op jit(solution)/shard_map/all_to_all | solution.py:213
  83.4 0.6 shard_map.52
  84.0 11.3 %all_to_all.40.got_ref = f32[8,16,128]{2,1,0:T(8,128)S(1)} all-to-all(f32[8,16,128]{2,1,0:T(8,128)S(1)} %get-tuple-element.11), channel_id=1, replica_groups=mesh['y2'=2,'y1'=2,'y0'=2,'z'=8,'x'=4,'c'=2] {'y2','y1','y0'}, dimensions={0} | all-to-all | bytes 131072 | tf_op jit(solution)/shard_map/all_to_all | solution.py:213
  95.2 9.5 %all_to_all.41.got_ref = f32[8,2,16,128]{3,2,1,0:T(8,128)S(1)} all-to-all(f32[8,2,16,128]{3,2,1,0:T(8,128)S(1)} %shard_map.53), channel_id=1, replica_groups=mesh['y2'=2,'y1'=2,'y0'=2,'z'=8,'x'=4,'c'=2] {'c','x'}, dimensions={0} | all-to-all | bytes 262144 | tf_op jit(solution)/shard_map/all_to_all | solution.py:213
  104.7 0.0 copy-done
  104.7 1.4 %shard_map.54 = f32[64,512]{1,0:T(8,128)} custom-call(f32[8,2,16,128]{3,2,1,0:T(8,128)S(1)} %all_to_all.41.got_ref, f32[1,3,512,256]{3,2,1,0:T(8,128)S(1)} %copy-done.1, f32[64,256]{1,0:T(8,128)S(1)} %get-tuple-element.10.coeff0_ref, f32[64,256]{1,0:T(8,128)S(1)} %get-tuple-element.12.coeff1_ref, f32[64,512]{1,0:T(8,128)S(1)} %copy-done.2, ...), custom_call_target="tpu_custom_call" | custom-call | tf_op jit(solution)/shard_map/pallas_call | solution.py:202
  (5 shorter events, 0.1 us)
Async XLA Ops:
  0.0 0.9 copy-start.2
  4.5 12.5 %collective-permute-start = (f32[4,8,32,128]{3,2,1,0:T(8,128)S(1)}, f32[4,8,32,128]{3,2,1,0:T(8,128)S(1)}, u32[]{:S(2)}, u32[]{:S(2)}) collective-permute-start(f32[4,8,32,128]{3,2,1,0:T(8,128)S(1)} %shard_map.47), channel_id=1, source_target_pairs={{0,1},{1,0},{2,3},{3,2},{4,5},{5,4},{6,7},{7,6},{8,9},{9,8},{10,11... | collective-permute-start | bytes 1572872 | tf_op jit(solution)/shard_map/ppermute | solution.py:224
  17.1 49.2 %copy-start.1 = (f32[1,3,512,256]{3,2,1,0:T(8,128)S(1)}, f32[1,3,512,256]{3,2,1,0:T(8,128)}, u32[]{:S(2)}) copy-start(f32[1,3,512,256]{3,2,1,0:T(8,128)} %core_ref.5) | copy-start | bytes 4718596
  66.9 37.9 %copy-start = (f32[3,256,512]{2,1,0:T(8,128)S(1)}, f32[3,256,512]{2,1,0:T(8,128)}, u32[]{:S(2)}) copy-start(f32[3,256,512]{2,1,0:T(8,128)} %left_ref.1) | copy-start | bytes 4718596

commit v3 on v2

--- a/solution.py
+++ b/solution.py
@@ -1,5 +1,3 @@
-import functools
-
 import jax
 import jax.numpy as jnp
 from jax import lax
@@ -34,10 +32,22 @@
     return product(halves(a), halves(b), ((1,), (1,)))
 
 
-def gram_kernel(own, field_hbm, right_hbm, left_hbm, out_ref, field, right, left, sems):
+def stacked_product(a_high, a_low, b):
+    rows = a_high.shape[0]
+
+    def one(u, v):
+        return lax.dot_general(u, v, (((1,), (1,)), ((), ())), preferred_element_type=jnp.float32)
+
+    both = one(jnp.concatenate([a_high, a_low], axis=0), b[0])
+    return both[:rows] + (both[rows:] + one(a_high, b[1]))
+
+
+def gram_kernel(field_hbm, right_hbm, left_hbm, theirs_ref, mine_ref, field, right, left, sems):
     core = lax.axis_index("c")
-    side = core if own else 1 - core
-    depth, _, rows = right.shape[:3]
+    sides = (1 - core, core)
+    outs = (theirs_ref, mine_ref)
+    depth, _, _, rows, points = right.shape
+    peers = mine_ref.shape[0]
     copies = []
 
     def fetch(src, dst):
@@ -46,63 +56,84 @@
         copies.append(copy)
         return copy
 
+    def fetch_right(k):
+        return [
+            fetch(right_hbm.at[k, pl.ds(2 * rows * h + rows * side, rows), :], right.at[k, slot, h])
+            for slot, side in enumerate(sides)
+            for h in range(2)
+        ]
+
+    def fetch_left(j):
+        part = left.shape[1] // 2
+        return [fetch(left_hbm.at[j, pl.ds(part * i, part), :], left.at[j, pl.ds(part * i, part), :]) for i in range(2)]
+
+    got_left, got_right = {}, {}
+    got_left[0] = fetch_left(0)
+    got_right[1] = fetch_right(1)
+    got_right[2] = fetch_right(2)
+    got_left[1] = fetch_left(1)
     got_field = fetch(field_hbm, field)
-    got_right = [
-        [fetch(right_hbm.at[k, pl.ds(2 * rows * h + rows * side, rows), :], right.at[k, h]) for h in range(2)]
-        for k in range(depth)
-    ]
-    got_left = [fetch(left_hbm.at[j], left.at[j]) for j in range(left.shape[0])]
-    peers = out_ref.shape[0]
-
-    def put_packed(block, row, value):
+    got_right[0] = fetch_right(0)
+
+    def arrived(waits):
+        for copy in waits:
+            copy.wait()
+
+    def basis(k):
+        arrived(got_right[k])
+        return halves(right[k].reshape(4 * rows, points))
+
+    def put(k, block, value):
+        for slot, out_ref in enumerate(outs):
+            for s in range(peers):
+                for h in range(2):
+                    first = 4 * rows * k + 2 * rows * slot + rows * h + HALF * s
+                    piece = value[first : first + HALF]
+                    out_ref[s, block, HALF * h : HALF * (h + 1), :] = piece[:, :LANES]
+                    out_ref[s, block + 1, HALF * h : HALF * (h + 1), :] = piece[:, LANES:]
+
+    def put_packed(k, value):
+        for slot, out_ref in enumerate(outs):
+            for s in range(peers):
+                first = 4 * rows * k + 2 * rows * slot + HALF * s
+                piece = [value[first + rows * h : first + rows * h + HALF] for h in range(2)]
+                out_ref[s, k // 2, HALF * (k % 2) : HALF * (k % 2 + 1), :] = jnp.concatenate(piece, axis=1)
+
+    for out_ref in outs:
         for s in range(peers):
-            top = value[HALF * s : HALF * (s + 1)]
-            low = value[rows + HALF * s : rows + HALF * (s + 1)]
-            out_ref[s, block, row : row + HALF, :] = jnp.concatenate([top, low], axis=1)
-
-    def put(block, value):
-        for s in range(peers):
-            for h in range(2):
-                out_ref[s, block, HALF * h : HALF * (h + 1), :] = value[
-                    rows * h + HALF * s : rows * h + HALF * (s + 1)
-                ]
-
-    for s in range(peers):
-        out_ref[s, 1, HALF:, :] = jnp.zeros((HALF, LANES), jnp.float32)
+            out_ref[s, 1, HALF:, :] = jnp.zeros((HALF, LANES), jnp.float32)
+    arrived(got_left[0])
+    first_left = halves(left[0])
+    one, two = basis(1), basis(2)
+    high, low = (jnp.concatenate([one[i], two[i]], axis=0) for i in range(2))
+    gram = stacked_product(high, low, first_left)
+    put(0, 2, gram)
+    put(1, 4, gram)
+    arrived(got_left[1])
+    put(0, 6, stacked_product(two[0], two[1], halves(left[1])))
     got_field.wait()
-    rhs = halves(field[...])
-    mine = []
+    zero = basis(0)
+    high, low = (jnp.concatenate([zero[i], one[i], two[i]], axis=0) for i in range(2))
+    proj = stacked_product(high, low, halves(field[...]))
     for k in range(depth):
-        for h in range(2):
-            got_right[k][h].wait()
-        mine.append(halves(right[k].reshape(2 * rows, right.shape[3])))
-        put_packed(k // 2, HALF * (k % 2), product(mine[k], rhs, ((1,), (1,))))
-    for j in range(left.shape[0]):
-        got_left[j].wait()
-        other = halves(left[j])
-        for k in range(j + 1, depth):
-            gram = product(mine[k], other, ((1,), (1,)))
-            block = 2 * (j + k)
-            put(block, gram[:, :LANES])
-            put(block + 1, gram[:, LANES:])
-
-
-def gram_rows(own, field, right, left):
+        put_packed(k, proj)
+
+
+def gram_rows(field, right, left):
     depth, rank, points = right.shape
     rows = rank // 4
-    scratch = [
-        pltpu.VMEM(field.shape, jnp.float32),
-        pltpu.VMEM((depth, 2, rows, points), jnp.float32),
-        pltpu.VMEM((depth - 1, rank, points), jnp.float32),
-        pltpu.SemaphoreType.DMA((1 + 2 * depth + depth - 1,)),
-    ]
+    out = jax.ShapeDtypeStruct((rows // HALF, BLOCKS, 2 * HALF, LANES), jnp.float32)
     return pl.pallas_call(
-        functools.partial(gram_kernel, own),
-        out_shape=jax.ShapeDtypeStruct((rows // HALF, BLOCKS, 2 * HALF, LANES), jnp.float32),
+        gram_kernel,
+        out_shape=(out, out),
         in_specs=[pl.BlockSpec(memory_space=pltpu.HBM)] * 3,
-        out_specs=pl.BlockSpec(memory_space=pltpu.VMEM),
-        scratch_shapes=scratch,
-        cost_estimate=pl.CostEstimate(flops=800_000_000, bytes_accessed=2_500_000, transcendentals=0),
+        out_specs=(pl.BlockSpec(memory_space=pltpu.VMEM),) * 2,
+        scratch_shapes=[
+            pltpu.VMEM(field.shape, jnp.float32),
+            pltpu.VMEM((depth, 2, 2, rows, points), jnp.float32),
+            pltpu.VMEM((depth - 1, rank, points), jnp.float32),
+            pltpu.SemaphoreType.DMA((1 + 4 * depth + 2 * (depth - 1),)),
+        ],
         compiler_params=pltpu.CompilerParams(vmem_limit_bytes=54000 << 10),
     )(field, right, left)
 
@@ -220,9 +251,8 @@
     half = (HALF, LANES)
     rhs, rank = rhs_field.shape[0], right_basis.shape[1]
 
-    theirs = gram_rows(False, rhs_field, right_basis, left_basis)
+    theirs, mine = gram_rows(rhs_field, right_basis, left_basis)
     theirs = lax.ppermute(theirs, "c", [(0, 1), (1, 0)])
-    mine = gram_rows(True, rhs_field, right_basis, left_basis)
     part = call(add_kernel, mine.shape, (mine, theirs))
     part = swap(part, "x")
     part = call(sum_kernel, (nz,) + tile, (part,))

time: 107 us -> 105 us (0.981)
  Pallas kernels: 9.94 us -> 6.72 us
  waiting for transfers between devices: 0.01 us -> 1.51 us
    pallas_call x2 -> x1, Pallas kernels: 7.31 us -> 4.09 us  [gram_rows(): pl.pallas_call(gram_kernel, out_shape=(out, out), in_specs=[pl.BlockSpec(...]
    ppermute x1, waiting for transfers between devices: 0.01 us -> 1.51 us  [shards(): theirs = lax.ppermute(theirs, 'c', [(0, 1), (1, 0)])]
  transfers between devices with their start and end apart: 1 -> 1, of which waited for: 0 -> 1; matrix products, arithmetic and copies ran while one was open for 0% -> 0% of each run, Pallas kernels for 3% -> 0%
where the time goes in v3:
time: 105 us; the launch traced here: 104 us
  blocking collectives  86.4 us (82%)
  starting transfers between devices  8.79 us (8%)
  Pallas kernels  6.72 us (6%)
  waiting for transfers between devices  1.51 us (1%)
    all_to_all x7, blocking collectives, swap(): return lax.all_to_all(x, axes, 0, 0, tiled=True)  86.4 us
    ppermute x1, starting transfers between devices, shards(): theirs = lax.ppermute(theirs, 'c', [(0, 1), (1, 0)])  8.79 us
    pallas_call x1, Pallas kernels, gram_rows(): pl.pallas_call(gram_kernel, out_shape=(out, out), in_specs=[pl.BlockSpec(...  4.09 us
    pallas_call x7, Pallas kernels, call(): pl.pallas_call(kernel, grid=(1,), out_shape=out[0] if single else out, in...  2.63 us
  transfers between devices with their start and end apart: 1, of which 1 were waited for; matrix products, arithmetic and copies ran while one was open for 0% of the time, Pallas kernels for 0%

profile of v3, /device:TPU:1, one launch (start us, length us, event | category | flops | bytes accessed | tf_op | source)
XLA Modules:
  0.0 104.4 jit_solution(1091389552425503103)
XLA Ops:
  0.0 0.0 copy-start.2
  0.0 0.9 copy-done.2
  0.9 4.1 %shard_map.46 = (f32[4,8,32,128]{3,2,1,0:T(8,128)S(1)}, f32[4,8,32,128]{3,2,1,0:T(8,128)S(1)}) custom-call(f32[64,512]{1,0:T(8,128)S(1)} %copy-done.2, f32[3,256,512]{2,1,0:T(8,128)} %right_hbm.1, f32[3,256,512]{2,1,0:T(8,128)} %left_ref.1), custom_call_target="tpu_custom_call" | custom-call | tf_op jit(solution)/shard_map/pallas_call | solution.py:126
  5.0 8.8 %collective-permute-start = (f32[4,8,32,128]{3,2,1,0:T(8,128)S(1)}, f32[4,8,32,128]{3,2,1,0:T(8,128)S(1)}, u32[]{:S(2)}, u32[]{:S(2)}) collective-permute-start(f32[4,8,32,128]{3,2,1,0:T(8,128)S(1)} %get-tuple-element.12), channel_id=1, source_target_pairs={{0,1},{1,0},{2,3},{3,2},{4,5},{5,4},{6,7},{7,6},{8,9},{9,8},{10,11... | collective-permute-start | bytes 1572872 | tf_op jit(solution)/shard_map/ppermute | solution.py:255
  13.8 1.5 %collective-permute-done.b_ref = f32[4,8,32,128]{3,2,1,0:T(8,128)S(1)} collective-permute-done((f32[4,8,32,128]{3,2,1,0:T(8,128)S(1)}, f32[4,8,32,128]{3,2,1,0:T(8,128)S(1)}, u32[]{:S(2)}, u32[]{:S(2)}) %collective-permute-start) | collective-permute-done | bytes 524320 | tf_op jit(solution)/shard_map/ppermute | solution.py:255
  15.3 0.1 shard_map.47
  15.4 0.0 copy-start
  15.4 11.8 %all_to_all.35.in_ref = f32[4,8,32,128]{3,2,1,0:T(8,128)S(1)} all-to-all(f32[4,8,32,128]{3,2,1,0:T(8,128)S(1)} %shard_map.47), channel_id=1, replica_groups=mesh['y2'=2,'y1'=2,'y0'=2,'z'=8,'x'=4,'c'=2] {'x'}, dimensions={0} | all-to-all | bytes 1048576 | tf_op jit(solution)/shard_map/all_to_all | solution.py:244
  27.2 13.3 %all_to_all.36.in_ref = f32[8,32,128]{2,1,0:T(8,128)S(1)} all-to-all(f32[8,32,128]{2,1,0:T(8,128)S(1)} %shard_map.48), channel_id=1, replica_groups=mesh['y2'=2,'y1'=2,'y0'=2,'z'=8,'x'=4,'c'=2] {'z'}, dimensions={0} | all-to-all | bytes 262144 | tf_op jit(solution)/shard_map/all_to_all | solution.py:244
  40.5 10.4 %all_to_all.37.blocks_ref = f32[8,32,128]{2,1,0:T(8,128)S(1)} all-to-all(f32[8,32,128]{2,1,0:T(8,128)S(1)} %shard_map.49), channel_id=1, replica_groups=mesh['y2'=2,'y1'=2,'y0'=2,'z'=8,'x'=4,'c'=2] {'z'}, dimensions={0} | all-to-all | bytes 262144 | tf_op jit(solution)/shard_map/all_to_all | solution.py:244
  50.9 13.6 %all_to_all.38 = f32[16,16,128]{2,1,0:T(8,128)S(1)} all-to-all(f32[16,16,128]{2,1,0:T(8,128)S(1)} %broadcast_in_dim.3), channel_id=1, replica_groups=mesh['y2'=2,'y1'=2,'y0'=2,'z'=8,'x'=4,'c'=2] {'y0','c','x'}, dimensions={0} | all-to-all | bytes 262144 | tf_op jit(solution)/shard_map/all_to_all | solution.py:244
  64.5 0.0 copy-done
  64.5 0.6 shard_map.50
  65.1 0.0 copy-start.1
  65.1 16.5 %all_to_all.39 = f32[32,16,128]{2,1,0:T(8,128)S(1)} all-to-all(f32[32,16,128]{2,1,0:T(8,128)S(1)} %get-tuple-element.13), channel_id=1, replica_groups=mesh['y2'=2,'y1'=2,'y0'=2,'z'=8,'x'=4,'c'=2] {'y1','y0','c','x'}, dimensions={0} | all-to-all | bytes 524288 | tf_op jit(solution)/shard_map/all_to_all | solution.py:244
  81.7 0.6 shard_map.51
  82.2 11.3 %all_to_all.40.got_ref = f32[8,16,128]{2,1,0:T(8,128)S(1)} all-to-all(f32[8,16,128]{2,1,0:T(8,128)S(1)} %get-tuple-element.15), channel_id=1, replica_groups=mesh['y2'=2,'y1'=2,'y0'=2,'z'=8,'x'=4,'c'=2] {'y2','y1','y0'}, dimensions={0} | all-to-all | bytes 131072 | tf_op jit(solution)/shard_map/all_to_all | solution.py:244
  93.5 9.5 %all_to_all.41.got_ref = f32[8,2,16,128]{3,2,1,0:T(8,128)S(1)} all-to-all(f32[8,2,16,128]{3,2,1,0:T(8,128)S(1)} %shard_map.52), channel_id=1, replica_groups=mesh['y2'=2,'y1'=2,'y0'=2,'z'=8,'x'=4,'c'=2] {'c','x'}, dimensions={0} | all-to-all | bytes 262144 | tf_op jit(solution)/shard_map/all_to_all | solution.py:244
  103.0 0.0 copy-done.1
  103.0 1.4 %shard_map.53 = f32[64,512]{1,0:T(8,128)} custom-call(f32[8,2,16,128]{3,2,1,0:T(8,128)S(1)} %all_to_all.41.got_ref, f32[1,3,512,256]{3,2,1,0:T(8,128)S(1)} %copy-done, f32[64,256]{1,0:T(8,128)S(1)} %get-tuple-element.14.coeff0_ref, f32[64,256]{1,0:T(8,128)S(1)} %get-tuple-element.16.coeff1_ref, f32[64,512]{1,0:T(8,128)S(1)} %copy-done.2, ...), custom_call_target="tpu_custom_call" | custom-call | tf_op jit(solution)/shard_map/pallas_call | solution.py:233
  (5 shorter events, 0.1 us)
Async XLA Ops:
  0.0 0.9 copy-start.2
  5.0 10.3 %collective-permute-start = (f32[4,8,32,128]{3,2,1,0:T(8,128)S(1)}, f32[4,8,32,128]{3,2,1,0:T(8,128)S(1)}, u32[]{:S(2)}, u32[]{:S(2)}) collective-permute-start(f32[4,8,32,128]{3,2,1,0:T(8,128)S(1)} %get-tuple-element.12), channel_id=1, source_target_pairs={{0,1},{1,0},{2,3},{3,2},{4,5},{5,4},{6,7},{7,6},{8,9},{9,8},{10,11... | collective-permute-start | bytes 1572872 | tf_op jit(solution)/shard_map/ppermute | solution.py:255
  15.4 49.2 %copy-start = (f32[1,3,512,256]{3,2,1,0:T(8,128)S(1)}, f32[1,3,512,256]{3,2,1,0:T(8,128)}, u32[]{:S(2)}) copy-start(f32[1,3,512,256]{3,2,1,0:T(8,128)} %core_ref.5) | copy-start | bytes 4718596
  65.1 37.9 %copy-start.1 = (f32[3,256,512]{2,1,0:T(8,128)S(1)}, f32[3,256,512]{2,1,0:T(8,128)}, u32[]{:S(2)}) copy-start(f32[3,256,512]{2,1,0:T(8,128)} %left_ref.1) | copy-start | bytes 4718596

commit v4 on v3

--- a/solution.py
+++ b/solution.py
@@ -142,13 +142,6 @@
     out_ref[...] = a_ref[...] + b_ref[...]
 
 
-def sum_kernel(in_ref, out_ref):
-    total = in_ref[0]
-    for s in range(1, in_ref.shape[0]):
-        total = total + in_ref[s]
-    out_ref[...] = total
-
-
 def sum_spread_kernel(in_ref, out_ref):
     total = in_ref[0]
     for s in range(1, in_ref.shape[0]):
@@ -254,9 +247,7 @@
     theirs, mine = gram_rows(rhs_field, right_basis, left_basis)
     theirs = lax.ppermute(theirs, "c", [(0, 1), (1, 0)])
     part = call(add_kernel, mine.shape, (mine, theirs))
-    part = swap(part, "x")
-    part = call(sum_kernel, (nz,) + tile, (part,))
-    part = swap(part, "z")
+    part = swap(part.reshape((nx * nz,) + tile), ("x", "z"))
     part = call(sum_spread_kernel, (nz,) + tile, (part,))
     blocks = swap(part, "z")
 

time: 105 us -> 104 us (level)
    all_to_all x7 -> x6, blocking collectives: 86.4 us -> 85.4 us  [swap(): return lax.all_to_all(x, axes, 0, 0, tiled=True)]
    pallas_call x7 -> x6, Pallas kernels: 2.63 us -> 2.63 us  [call(): pl.pallas_call(kernel, grid=(1,), out_shape=out[0] if single else out, in...]
where the time goes in v4:
time: 104 us; the launch traced here: 103 us
  blocking collectives  85.4 us (82%)
  starting transfers between devices  8.79 us (8%)
  Pallas kernels  6.72 us (6%)
  waiting for transfers between devices  1.51 us (1%)
    all_to_all x6, blocking collectives, swap(): return lax.all_to_all(x, axes, 0, 0, tiled=True)  85.4 us
    ppermute x1, starting transfers between devices, shards(): theirs = lax.ppermute(theirs, 'c', [(0, 1), (1, 0)])  8.79 us
    pallas_call x1, Pallas kernels, gram_rows(): pl.pallas_call(gram_kernel, out_shape=(out, out), in_specs=[pl.BlockSpec(...  4.09 us
    pallas_call x6, Pallas kernels, call(): pl.pallas_call(kernel, grid=(1,), out_shape=out[0] if single else out, in...  2.63 us
  transfers between devices with their start and end apart: 1, of which 1 were waited for; matrix products, arithmetic and copies ran while one was open for 0% of the time, Pallas kernels for 0%

profile of v4, /device:TPU:1, one launch (start us, length us, event | category | flops | bytes accessed | tf_op | source)
XLA Modules:
  0.0 103.4 jit_solution(8877301708973352228)
XLA Ops:
  0.0 0.0 copy-start.2
  0.0 0.9 copy-done.2
  0.9 4.1 %shard_map.46 = (f32[4,8,32,128]{3,2,1,0:T(8,128)S(1)}, f32[4,8,32,128]{3,2,1,0:T(8,128)S(1)}) custom-call(f32[64,512]{1,0:T(8,128)S(1)} %copy-done.2, f32[3,256,512]{2,1,0:T(8,128)} %right_hbm.1, f32[3,256,512]{2,1,0:T(8,128)} %left_ref.1), custom_call_target="tpu_custom_call" | custom-call | tf_op jit(solution)/shard_map/pallas_call | solution.py:126
  5.0 8.8 %collective-permute-start = (f32[4,8,32,128]{3,2,1,0:T(8,128)S(1)}, f32[4,8,32,128]{3,2,1,0:T(8,128)S(1)}, u32[]{:S(2)}, u32[]{:S(2)}) collective-permute-start(f32[4,8,32,128]{3,2,1,0:T(8,128)S(1)} %get-tuple-element.12), channel_id=1, source_target_pairs={{0,1},{1,0},{2,3},{3,2},{4,5},{5,4},{6,7},{7,6},{8,9},{9,8},{10,11... | collective-permute-start | bytes 1572872 | tf_op jit(solution)/shard_map/ppermute | solution.py:248
  13.8 1.5 %collective-permute-done.b_ref = f32[4,8,32,128]{3,2,1,0:T(8,128)S(1)} collective-permute-done((f32[4,8,32,128]{3,2,1,0:T(8,128)S(1)}, f32[4,8,32,128]{3,2,1,0:T(8,128)S(1)}, u32[]{:S(2)}, u32[]{:S(2)}) %collective-permute-start) | collective-permute-done | bytes 524320 | tf_op jit(solution)/shard_map/ppermute | solution.py:248
  15.3 0.1 shard_map.47
  15.4 0.0 copy-start
  15.4 21.6 %all_to_all.30.in_ref = f32[32,32,128]{2,1,0:T(8,128)S(1)} all-to-all(f32[32,32,128]{2,1,0:T(8,128)S(1)} %bitcast.5), channel_id=1, replica_groups=mesh['y2'=2,'y1'=2,'y0'=2,'z'=8,'x'=4,'c'=2] {'x','z'}, dimensions={0} | all-to-all | bytes 1048576 | tf_op jit(solution)/shard_map/all_to_all | solution.py:237
  37.0 14.0 %all_to_all.31.blocks_ref = f32[8,32,128]{2,1,0:T(8,128)S(1)} all-to-all(f32[8,32,128]{2,1,0:T(8,128)S(1)} %shard_map.48), channel_id=1, replica_groups=mesh['y2'=2,'y1'=2,'y0'=2,'z'=8,'x'=4,'c'=2] {'z'}, dimensions={0} | all-to-all | bytes 262144 | tf_op jit(solution)/shard_map/all_to_all | solution.py:237
  51.1 12.6 %all_to_all.32 = f32[16,16,128]{2,1,0:T(8,128)S(1)} all-to-all(f32[16,16,128]{2,1,0:T(8,128)S(1)} %broadcast_in_dim.3), channel_id=1, replica_groups=mesh['y2'=2,'y1'=2,'y0'=2,'z'=8,'x'=4,'c'=2] {'y0','c','x'}, dimensions={0} | all-to-all | bytes 262144 | tf_op jit(solution)/shard_map/all_to_all | solution.py:237
  63.6 0.0 copy-done
  63.6 0.6 shard_map.49
  64.2 0.0 copy-start.1
  64.2 16.5 %all_to_all.33 = f32[32,16,128]{2,1,0:T(8,128)S(1)} all-to-all(f32[32,16,128]{2,1,0:T(8,128)S(1)} %get-tuple-element.13), channel_id=1, replica_groups=mesh['y2'=2,'y1'=2,'y0'=2,'z'=8,'x'=4,'c'=2] {'y1','y0','c','x'}, dimensions={0} | all-to-all | bytes 524288 | tf_op jit(solution)/shard_map/all_to_all | solution.py:237
  80.8 0.6 shard_map.50
  81.3 11.2 %all_to_all.34.got_ref = f32[8,16,128]{2,1,0:T(8,128)S(1)} all-to-all(f32[8,16,128]{2,1,0:T(8,128)S(1)} %get-tuple-element.15), channel_id=1, replica_groups=mesh['y2'=2,'y1'=2,'y0'=2,'z'=8,'x'=4,'c'=2] {'y2','y1','y0'}, dimensions={0} | all-to-all | bytes 131072 | tf_op jit(solution)/shard_map/all_to_all | solution.py:237
  92.5 9.5 %all_to_all.35.got_ref = f32[8,2,16,128]{3,2,1,0:T(8,128)S(1)} all-to-all(f32[8,2,16,128]{3,2,1,0:T(8,128)S(1)} %shard_map.51), channel_id=1, replica_groups=mesh['y2'=2,'y1'=2,'y0'=2,'z'=8,'x'=4,'c'=2] {'c','x'}, dimensions={0} | all-to-all | bytes 262144 | tf_op jit(solution)/shard_map/all_to_all | solution.py:237
  102.0 0.0 copy-done.1
  102.0 1.4 %shard_map.52 = f32[64,512]{1,0:T(8,128)} custom-call(f32[8,2,16,128]{3,2,1,0:T(8,128)S(1)} %all_to_all.35.got_ref, f32[1,3,512,256]{3,2,1,0:T(8,128)S(1)} %copy-done, f32[64,256]{1,0:T(8,128)S(1)} %get-tuple-element.14.coeff0_ref, f32[64,256]{1,0:T(8,128)S(1)} %get-tuple-element.16.coeff1_ref, f32[64,512]{1,0:T(8,128)S(1)} %copy-done.2, ...), custom_call_target="tpu_custom_call" | custom-call | tf_op jit(solution)/shard_map/pallas_call | solution.py:226
  (4 shorter events, 0.1 us)
Async XLA Ops:
  0.0 0.9 copy-start.2
  5.0 10.3 %collective-permute-start = (f32[4,8,32,128]{3,2,1,0:T(8,128)S(1)}, f32[4,8,32,128]{3,2,1,0:T(8,128)S(1)}, u32[]{:S(2)}, u32[]{:S(2)}) collective-permute-start(f32[4,8,32,128]{3,2,1,0:T(8,128)S(1)} %get-tuple-element.12), channel_id=1, source_target_pairs={{0,1},{1,0},{2,3},{3,2},{4,5},{5,4},{6,7},{7,6},{8,9},{9,8},{10,11... | collective-permute-start | bytes 1572872 | tf_op jit(solution)/shard_map/ppermute | solution.py:248
  15.4 48.3 %copy-start = (f32[1,3,512,256]{3,2,1,0:T(8,128)S(1)}, f32[1,3,512,256]{3,2,1,0:T(8,128)}, u32[]{:S(2)}) copy-start(f32[1,3,512,256]{3,2,1,0:T(8,128)} %core_ref.5) | copy-start | bytes 4718596
  64.2 37.8 %copy-start.1 = (f32[3,256,512]{2,1,0:T(8,128)S(1)}, f32[3,256,512]{2,1,0:T(8,128)}, u32[]{:S(2)}) copy-start(f32[3,256,512]{2,1,0:T(8,128)} %left_ref.1) | copy-start | bytes 4718596

commit v5 on v4

--- a/solution.py
+++ b/solution.py
@@ -47,7 +47,7 @@
     sides = (1 - core, core)
     outs = (theirs_ref, mine_ref)
     depth, _, _, rows, points = right.shape
-    peers = mine_ref.shape[0]
+    peers = mine_ref.shape[1]
     copies = []
 
     def fetch(src, dst):
@@ -89,19 +89,19 @@
                 for h in range(2):
                     first = 4 * rows * k + 2 * rows * slot + rows * h + HALF * s
                     piece = value[first : first + HALF]
-                    out_ref[s, block, HALF * h : HALF * (h + 1), :] = piece[:, :LANES]
-                    out_ref[s, block + 1, HALF * h : HALF * (h + 1), :] = piece[:, LANES:]
+                    out_ref[block, s, HALF * h : HALF * (h + 1), :] = piece[:, :LANES]
+                    out_ref[block + 1, s, HALF * h : HALF * (h + 1), :] = piece[:, LANES:]
 
     def put_packed(k, value):
         for slot, out_ref in enumerate(outs):
             for s in range(peers):
                 first = 4 * rows * k + 2 * rows * slot + HALF * s
                 piece = [value[first + rows * h : first + rows * h + HALF] for h in range(2)]
-                out_ref[s, k // 2, HALF * (k % 2) : HALF * (k % 2 + 1), :] = jnp.concatenate(piece, axis=1)
+                out_ref[k // 2, s, HALF * (k % 2) : HALF * (k % 2 + 1), :] = jnp.concatenate(piece, axis=1)
 
     for out_ref in outs:
         for s in range(peers):
-            out_ref[s, 1, HALF:, :] = jnp.zeros((HALF, LANES), jnp.float32)
+            out_ref[1, s, HALF:, :] = jnp.zeros((HALF, LANES), jnp.float32)
     arrived(got_left[0])
     first_left = halves(left[0])
     one, two = basis(1), basis(2)
@@ -122,7 +122,7 @@
 def gram_rows(field, right, left):
     depth, rank, points = right.shape
     rows = rank // 4
-    out = jax.ShapeDtypeStruct((rows // HALF, BLOCKS, 2 * HALF, LANES), jnp.float32)
+    out = jax.ShapeDtypeStruct((BLOCKS, rows // HALF, 2 * HALF, LANES), jnp.float32)
     return pl.pallas_call(
         gram_kernel,
         out_shape=(out, out),
@@ -170,9 +170,12 @@
 
 
 def quads_kernel(got_ref, out_ref):
-    for side, part in enumerate(two_sides(got_ref)):
-        for s in range(out_ref.shape[0]):
-            out_ref[s, side] = part
+    group = got_ref.shape[1] // 2
+    for side in range(2):
+        part = got_ref[:, side * group]
+        for g in range(1, group):
+            part = part + got_ref[:, side * group + g]
+        out_ref[side] = part
 
 
 def packed(value):
@@ -201,11 +204,19 @@
         out_ref[s] = fresh
 
 
-def level2_kernel(got_ref, core_ref, coeff0_ref, coeff1_ref, field_ref, left_ref, out_ref):
+def base_kernel(coeff0_ref, coeff1_ref, field_ref, left_ref, out_ref):
     change = mul(coeff0_ref[...], left_ref[0]) + mul(coeff1_ref[...], left_ref[1])
-    coeff = coefficients([got_ref[:, 0], got_ref[:, 1]], core_ref)
-    change = change + mul(coeff, left_ref[2])
     out_ref[...] = field_ref[...] - change
+
+
+def level2_kernel(mine_ref, theirs_ref, core_ref, base_ref, left_ref, out_ref):
+    first = lax.axis_index("c") == 0
+    parts = []
+    for side in range(2):
+        mine, theirs = mine_ref[side], theirs_ref[side]
+        parts.append(jnp.stack([jnp.where(first, mine, theirs), jnp.where(first, theirs, mine)]))
+    coeff = coefficients(parts, core_ref)
+    out_ref[...] = base_ref[...] - mul(coeff, left_ref[0])
 
 
 def whole(x):
@@ -214,6 +225,10 @@
 
 def core_of(cores, level):
     return pl.BlockSpec((1, 1) + cores.shape[2:], lambda i: (0, level, 0, 0))
+
+
+def levels_of(basis, first, count):
+    return pl.BlockSpec((count,) + basis.shape[1:], lambda i: (first // count, 0, 0))
 
 
 def call(kernel, out_shape, args, in_specs=None):
@@ -247,7 +262,7 @@
     theirs, mine = gram_rows(rhs_field, right_basis, left_basis)
     theirs = lax.ppermute(theirs, "c", [(0, 1), (1, 0)])
     part = call(add_kernel, mine.shape, (mine, theirs))
-    part = swap(part.reshape((nx * nz,) + tile), ("x", "z"))
+    part = swap(part.reshape((nz * nx,) + tile), ("z", "x"))
     part = call(sum_spread_kernel, (nz,) + tile, (part,))
     blocks = swap(part, "z")
 
@@ -262,18 +277,24 @@
     got = swap(send, ("y1", "y0") + CHIP).reshape((4, ns) + half)
     coeff1, send = call(
         level1_kernel,
-        ((rhs, rank), (8,) + half),
+        ((rhs, rank), (8 * nx,) + half),
         (got, cores, blocks, coeff0),
         [whole(got), core_of(cores, 1), whole(blocks), whole(coeff0)],
     )
-    got = swap(send, LEAF)
-    send = call(quads_kernel, (ns, 2) + half, (got,))
-    got = swap(send, CHIP)
+    got = swap(send, ("x",) + LEAF).reshape((nx, 8) + half)
+    mine = call(quads_kernel, (2, nx) + half, (got,))
+    theirs = lax.ppermute(mine, "c", [(0, 1), (1, 0)])
+    base = call(
+        base_kernel,
+        rhs_field.shape,
+        (coeff0, coeff1, rhs_field, left_basis),
+        [whole(coeff0), whole(coeff1), whole(rhs_field), levels_of(left_basis, 0, 2)],
+    )
     return call(
         level2_kernel,
         rhs_field.shape,
-        (got, cores, coeff0, coeff1, rhs_field, left_basis),
-        [whole(got), core_of(cores, 2), whole(coeff0), whole(coeff1), whole(rhs_field), whole(left_basis)],
+        (mine, theirs, cores, base, left_basis),
+        [whole(mine), whole(theirs), core_of(cores, 2), whole(base), levels_of(left_basis, 2, 1)],
     )
 
 

time: 104 us -> 104 us (level)
  blocking collectives: 85.4 us -> 79.1 us
  starting transfers between devices: 8.79 us -> 14.3 us
    all_to_all x6 -> x5, blocking collectives: 85.4 us -> 79.1 us  [swap(): return lax.all_to_all(x, axes, 0, 0, tiled=True)]
    ppermute x0 -> x1, starting transfers between devices: none -> 5.53 us  [shards(): theirs = lax.ppermute(mine, 'c', [(0, 1), (1, 0)])]
    pallas_call x6 -> x7, Pallas kernels: 2.63 us -> 3.08 us  [call(): pl.pallas_call(kernel, grid=(1,), out_shape=out[0] if single else out, in...]
  transfers between devices with their start and end apart: 1 -> 2, of which waited for: 1 -> 2; matrix products, arithmetic and copies ran while one was open for 0% -> 0% of each run, Pallas kernels for 0% -> 0%
where the time goes in v5:
time: 104 us
  blocking collectives  79.1 us (76%)
  starting transfers between devices  14.3 us (14%)
  Pallas kernels  7.17 us (7%)
  waiting for transfers between devices  1.96 us (2%)
    all_to_all x5, blocking collectives, swap(): return lax.all_to_all(x, axes, 0, 0, tiled=True)  79.1 us
    ppermute x1, starting transfers between devices, shards(): theirs = lax.ppermute(theirs, 'c', [(0, 1), (1, 0)])  8.79 us
    ppermute x1, starting transfers between devices, shards(): theirs = lax.ppermute(mine, 'c', [(0, 1), (1, 0)])  5.53 us
    pallas_call x1, Pallas kernels, gram_rows(): pl.pallas_call(gram_kernel, out_shape=(out, out), in_specs=[pl.BlockSpec(...  4.09 us
    pallas_call x7, Pallas kernels, call(): pl.pallas_call(kernel, grid=(1,), out_shape=out[0] if single else out, in...  3.08 us
  transfers between devices with their start and end apart: 2, of which 2 were waited for; matrix products, arithmetic and copies ran while one was open for 0% of the time, Pallas kernels for 0%

profile of v5, /device:TPU:1, one launch (start us, length us, event | category | flops | bytes accessed | tf_op | source)
XLA Modules:
  0.0 103.6 jit_solution(8770095463413595278)
XLA Ops:
  0.0 0.0 copy-start.2
  0.0 0.9 copy-done.2
  0.9 4.1 %shard_map.46 = (f32[8,4,32,128]{3,2,1,0:T(8,128)S(1)}, f32[8,4,32,128]{3,2,1,0:T(8,128)S(1)}) custom-call(f32[64,512]{1,0:T(8,128)S(1)} %copy-done.2, f32[3,256,512]{2,1,0:T(8,128)} %right_hbm.1, f32[3,256,512]{2,1,0:T(8,128)} %left_ref.3), custom_call_target="tpu_custom_call" | custom-call | tf_op jit(solution)/shard_map/pallas_call | solution.py:126
  5.0 8.8 %collective-permute-start = (f32[8,4,32,128]{3,2,1,0:T(8,128)S(1)}, f32[8,4,32,128]{3,2,1,0:T(8,128)S(1)}, u32[]{:S(2)}, u32[]{:S(2)}) collective-permute-start(f32[8,4,32,128]{3,2,1,0:T(8,128)S(1)} %get-tuple-element.12), channel_id=1, source_target_pairs={{0,1},{1,0},{2,3},{3,2},{4,5},{5,4},{6,7},{7,6},{8,9},{9,8},{10,11... | collective-permute-start | bytes 1572872 | tf_op jit(solution)/shard_map/ppermute | solution.py:263
  13.8 1.5 %collective-permute-done.b_ref = f32[8,4,32,128]{3,2,1,0:T(8,128)S(1)} collective-permute-done((f32[8,4,32,128]{3,2,1,0:T(8,128)S(1)}, f32[8,4,32,128]{3,2,1,0:T(8,128)S(1)}, u32[]{:S(2)}, u32[]{:S(2)}) %collective-permute-start) | collective-permute-done | bytes 524320 | tf_op jit(solution)/shard_map/ppermute | solution.py:263
  15.3 0.1 shard_map.47
  15.4 0.0 copy-start.1
  15.4 24.0 %all_to_all.25.in_ref = f32[32,32,128]{2,1,0:T(8,128)S(1)} all-to-all(f32[32,32,128]{2,1,0:T(8,128)S(1)} %bitcast.6), channel_id=1, replica_groups=mesh['y2'=2,'y1'=2,'y0'=2,'z'=8,'x'=4,'c'=2] {'z','x'}, dimensions={0} | all-to-all | bytes 1048576 | tf_op jit(solution)/shard_map/all_to_all | solution.py:252
  39.5 11.7 %all_to_all.26.blocks_ref = f32[8,32,128]{2,1,0:T(8,128)S(1)} all-to-all(f32[8,32,128]{2,1,0:T(8,128)S(1)} %shard_map.48), channel_id=1, replica_groups=mesh['y2'=2,'y1'=2,'y0'=2,'z'=8,'x'=4,'c'=2] {'z'}, dimensions={0} | all-to-all | bytes 262144 | tf_op jit(solution)/shard_map/all_to_all | solution.py:252
  51.2 12.5 %all_to_all.27 = f32[16,16,128]{2,1,0:T(8,128)S(1)} all-to-all(f32[16,16,128]{2,1,0:T(8,128)S(1)} %broadcast_in_dim.3), channel_id=1, replica_groups=mesh['y2'=2,'y1'=2,'y0'=2,'z'=8,'x'=4,'c'=2] {'y0','c','x'}, dimensions={0} | all-to-all | bytes 262144 | tf_op jit(solution)/shard_map/all_to_all | solution.py:252
  63.7 0.0 copy-done.1
  63.7 0.6 shard_map.49
  64.3 16.4 %all_to_all.28 = f32[32,16,128]{2,1,0:T(8,128)S(1)} all-to-all(f32[32,16,128]{2,1,0:T(8,128)S(1)} %get-tuple-element.13), channel_id=1, replica_groups=mesh['y2'=2,'y1'=2,'y0'=2,'z'=8,'x'=4,'c'=2] {'y1','y0','c','x'}, dimensions={0} | all-to-all | bytes 524288 | tf_op jit(solution)/shard_map/all_to_all | solution.py:252
  80.7 0.0 copy-start
  80.7 0.6 shard_map.50
  81.3 14.5 %all_to_all.29 = f32[32,16,128]{2,1,0:T(8,128)S(1)} all-to-all(f32[32,16,128]{2,1,0:T(8,128)S(1)} %get-tuple-element.15), channel_id=1, replica_groups=mesh['y2'=2,'y1'=2,'y0'=2,'z'=8,'x'=4,'c'=2] {'x','y2','y1','y0'}, dimensions={0} | all-to-all | bytes 524288 | tf_op jit(solution)/shard_map/all_to_all | solution.py:252
  95.8 5.5 %collective-permute-start.1 = (f32[2,4,16,128]{3,2,1,0:T(8,128)S(1)}, f32[2,4,16,128]{3,2,1,0:T(8,128)S(1)}, u32[]{:S(2)}, u32[]{:S(2)}) collective-permute-start(f32[2,4,16,128]{3,2,1,0:T(8,128)S(1)} %shard_map.51.mine_ref), channel_id=1, source_target_pairs={{0,1},{1,0},{2,3},{3,2},{4,5},{5,4},{6,7},{7,6},{8,9},{9,8},{10,11... | collective-permute-start | bytes 196616 | tf_op jit(solution)/shard_map/ppermute | solution.py:286
  101.3 0.0 copy-done
  101.3 0.4 shard_map.52.base_ref
  101.7 0.4 collective-permute-done.1.theirs_ref
  102.2 1.4 %shard_map.53 = f32[64,512]{1,0:T(8,128)} custom-call(f32[2,4,16,128]{3,2,1,0:T(8,128)S(1)} %shard_map.51.mine_ref, f32[2,4,16,128]{3,2,1,0:T(8,128)S(1)} %collective-permute-done.1.theirs_ref, f32[1,3,512,256]{3,2,1,0:T(8,128)S(1)} %copy-done.1, f32[64,512]{1,0:T(8,128)S(1)} %shard_map.52.base_ref, f32[3,256,512]{2,1,0:T(8,128)S(1)} %copy-done), custom_call_target="tpu_custom_call" | custom-call | tf_op jit(solution)/shard_map/pallas_call | solution.py:241
  (4 shorter events, 0.1 us)
Async XLA Ops:
  0.0 0.9 copy-start.2
  5.0 10.3 %collective-permute-start = (f32[8,4,32,128]{3,2,1,0:T(8,128)S(1)}, f32[8,4,32,128]{3,2,1,0:T(8,128)S(1)}, u32[]{:S(2)}, u32[]{:S(2)}) collective-permute-start(f32[8,4,32,128]{3,2,1,0:T(8,128)S(1)} %get-tuple-element.12), channel_id=1, source_target_pairs={{0,1},{1,0},{2,3},{3,2},{4,5},{5,4},{6,7},{7,6},{8,9},{9,8},{10,11... | collective-permute-start | bytes 1572872 | tf_op jit(solution)/shard_map/ppermute | solution.py:263
  15.4 48.3 %copy-start.1 = (f32[1,3,512,256]{3,2,1,0:T(8,128)S(1)}, f32[1,3,512,256]{3,2,1,0:T(8,128)}, u32[]{:S(2)}) copy-start(f32[1,3,512,256]{3,2,1,0:T(8,128)} %core_ref.5) | copy-start | bytes 4718596
  80.7 20.6 %copy-start = (f32[3,256,512]{2,1,0:T(8,128)S(1)}, f32[3,256,512]{2,1,0:T(8,128)}, u32[]{:S(2)}) copy-start(f32[3,256,512]{2,1,0:T(8,128)} %left_ref.3) | copy-start | bytes 4718596
  95.8 6.4 %collective-permute-start.1 = (f32[2,4,16,128]{3,2,1,0:T(8,128)S(1)}, f32[2,4,16,128]{3,2,1,0:T(8,128)S(1)}, u32[]{:S(2)}, u32[]{:S(2)}) collective-permute-start(f32[2,4,16,128]{3,2,1,0:T(8,128)S(1)} %shard_map.51.mine_ref), channel_id=1, source_target_pairs={{0,1},{1,0},{2,3},{3,2},{4,5},{5,4},{6,7},{7,6},{8,9},{9,8},{10,11... | collective-permute-start | bytes 196616 | tf_op jit(solution)/shard_map/ppermute | solution.py:286

commit v6 on v4

--- a/solution.py
+++ b/solution.py
@@ -21,7 +21,13 @@
     def one(u, v):
         return lax.dot_general(u, v, (dims, ((), ())), preferred_element_type=jnp.float32)
 
-    return one(a[0], b[0]) + (one(a[0], b[1]) + one(a[1], b[0]))
+    rows = a[0].shape[0]
+    both = one(jnp.concatenate(a, axis=0), b[0])
+    return both[:rows] + (both[rows:] + one(a[0], b[1]))
+
+
+def product_t(a, b):
+    return product(a, b, ((1,), (1,)))
 
 
 def mul(a, b):
@@ -29,100 +35,74 @@
 
 
 def mul_t(a, b):
-    return product(halves(a), halves(b), ((1,), (1,)))
-
-
-def stacked_product(a_high, a_low, b):
-    rows = a_high.shape[0]
-
-    def one(u, v):
-        return lax.dot_general(u, v, (((1,), (1,)), ((), ())), preferred_element_type=jnp.float32)
-
-    both = one(jnp.concatenate([a_high, a_low], axis=0), b[0])
-    return both[:rows] + (both[rows:] + one(a_high, b[1]))
+    return product_t(halves(a), halves(b))
 
 
 def gram_kernel(field_hbm, right_hbm, left_hbm, theirs_ref, mine_ref, field, right, left, sems):
-    core = lax.axis_index("c")
-    sides = (1 - core, core)
-    outs = (theirs_ref, mine_ref)
-    depth, _, _, rows, points = right.shape
-    peers = mine_ref.shape[0]
+    first_core = lax.axis_index("c") == 0
+    depth, rank, _ = right.shape
+    rows = rank // 4
+    peers = mine_ref.shape[1]
     copies = []
 
     def fetch(src, dst):
         copy = pltpu.make_async_copy(src, dst, sems.at[len(copies)])
         copy.start()
         copies.append(copy)
-        return copy
-
-    def fetch_right(k):
-        return [
-            fetch(right_hbm.at[k, pl.ds(2 * rows * h + rows * side, rows), :], right.at[k, slot, h])
-            for slot, side in enumerate(sides)
-            for h in range(2)
-        ]
-
-    def fetch_left(j):
-        part = left.shape[1] // 2
-        return [fetch(left_hbm.at[j, pl.ds(part * i, part), :], left.at[j, pl.ds(part * i, part), :]) for i in range(2)]
-
-    got_left, got_right = {}, {}
-    got_left[0] = fetch_left(0)
-    got_right[1] = fetch_right(1)
-    got_right[2] = fetch_right(2)
-    got_left[1] = fetch_left(1)
-    got_field = fetch(field_hbm, field)
-    got_right[0] = fetch_right(0)
-
-    def arrived(waits):
-        for copy in waits:
+
+    fetch(left_hbm.at[0], left.at[0])
+    fetch(right_hbm.at[1], right.at[1])
+    fetch(right_hbm.at[2], right.at[2])
+    fetch(left_hbm.at[1], left.at[1])
+    fetch(field_hbm, field)
+    fetch(right_hbm.at[0], right.at[0])
+
+    def arrived(group):
+        for copy in group:
             copy.wait()
 
     def basis(k):
-        arrived(got_right[k])
-        return halves(right[k].reshape(4 * rows, points))
-
-    def put(k, block, value):
-        for slot, out_ref in enumerate(outs):
-            for s in range(peers):
-                for h in range(2):
-                    first = 4 * rows * k + 2 * rows * slot + rows * h + HALF * s
-                    piece = value[first : first + HALF]
-                    out_ref[s, block, HALF * h : HALF * (h + 1), :] = piece[:, :LANES]
-                    out_ref[s, block + 1, HALF * h : HALF * (h + 1), :] = piece[:, LANES:]
+        return halves(right[k])
+
+    def pieces(value, s, h):
+        first = 2 * rows * h + HALF * s
+        zero, one = value[first : first + HALF], value[first + rows : first + rows + HALF]
+        return jnp.where(first_core, zero, one), jnp.where(first_core, one, zero)
+
+    def put(block, value):
+        for s in range(peers):
+            for h in range(2):
+                for out_ref, piece in zip((mine_ref, theirs_ref), pieces(value, s, h)):
+                    out_ref[block, s, HALF * h : HALF * (h + 1), :] = piece[:, :LANES]
+                    out_ref[block + 1, s, HALF * h : HALF * (h + 1), :] = piece[:, LANES:]
 
     def put_packed(k, value):
-        for slot, out_ref in enumerate(outs):
-            for s in range(peers):
-                first = 4 * rows * k + 2 * rows * slot + HALF * s
-                piece = [value[first + rows * h : first + rows * h + HALF] for h in range(2)]
-                out_ref[s, k // 2, HALF * (k % 2) : HALF * (k % 2 + 1), :] = jnp.concatenate(piece, axis=1)
-
-    for out_ref in outs:
         for s in range(peers):
-            out_ref[s, 1, HALF:, :] = jnp.zeros((HALF, LANES), jnp.float32)
-    arrived(got_left[0])
-    first_left = halves(left[0])
-    one, two = basis(1), basis(2)
-    high, low = (jnp.concatenate([one[i], two[i]], axis=0) for i in range(2))
-    gram = stacked_product(high, low, first_left)
-    put(0, 2, gram)
-    put(1, 4, gram)
-    arrived(got_left[1])
-    put(0, 6, stacked_product(two[0], two[1], halves(left[1])))
-    got_field.wait()
-    zero = basis(0)
-    high, low = (jnp.concatenate([zero[i], one[i], two[i]], axis=0) for i in range(2))
-    proj = stacked_product(high, low, halves(field[...]))
-    for k in range(depth):
-        put_packed(k, proj)
+            both = zip(pieces(value, s, 0), pieces(value, s, 1))
+            for out_ref, piece in zip((mine_ref, theirs_ref), both):
+                out_ref[k // 2, s, HALF * (k % 2) : HALF * (k % 2 + 1), :] = jnp.concatenate(piece, axis=1)
+
+    for out_ref in (mine_ref, theirs_ref):
+        for s in range(peers):
+            out_ref[1, s, HALF:, :] = jnp.zeros((HALF, LANES), jnp.float32)
+    arrived(copies[:3])
+    left_0 = halves(left[0])
+    right_1 = basis(1)
+    put(2, product_t(right_1, left_0))
+    right_2 = basis(2)
+    put(4, product_t(right_2, left_0))
+    arrived(copies[3:])
+    put(6, product_t(right_2, halves(left[1])))
+    rhs = halves(field[...])
+    put_packed(1, product_t(right_1, rhs))
+    put_packed(2, product_t(right_2, rhs))
+    put_packed(0, product_t(basis(0), rhs))
 
 
 def gram_rows(field, right, left):
     depth, rank, points = right.shape
     rows = rank // 4
-    out = jax.ShapeDtypeStruct((rows // HALF, BLOCKS, 2 * HALF, LANES), jnp.float32)
+    out = jax.ShapeDtypeStruct((BLOCKS, rows // HALF, 2 * HALF, LANES), jnp.float32)
     return pl.pallas_call(
         gram_kernel,
         out_shape=(out, out),
@@ -130,9 +110,9 @@
         out_specs=(pl.BlockSpec(memory_space=pltpu.VMEM),) * 2,
         scratch_shapes=[
             pltpu.VMEM(field.shape, jnp.float32),
-            pltpu.VMEM((depth, 2, 2, rows, points), jnp.float32),
+            pltpu.VMEM((depth, rank, points), jnp.float32),
             pltpu.VMEM((depth - 1, rank, points), jnp.float32),
-            pltpu.SemaphoreType.DMA((1 + 4 * depth + 2 * (depth - 1),)),
+            pltpu.SemaphoreType.DMA((2 * depth,)),
         ],
         compiler_params=pltpu.CompilerParams(vmem_limit_bytes=54000 << 10),
     )(field, right, left)
@@ -247,7 +227,7 @@
     theirs, mine = gram_rows(rhs_field, right_basis, left_basis)
     theirs = lax.ppermute(theirs, "c", [(0, 1), (1, 0)])
     part = call(add_kernel, mine.shape, (mine, theirs))
-    part = swap(part.reshape((nx * nz,) + tile), ("x", "z"))
+    part = swap(part.reshape((nz * nx,) + tile), ("z", "x"))
     part = call(sum_spread_kernel, (nz,) + tile, (part,))
     blocks = swap(part, "z")
 

time: 104 us -> 103 us (level)
  Pallas kernels: 6.72 us -> 5.4 us
where the time goes in v6:
time: 103 us; the launch traced here: 102 us
  blocking collectives  85.5 us (83%)
  starting transfers between devices  8.79 us (9%)
  Pallas kernels  5.4 us (5%)
  waiting for transfers between devices  1.51 us (1%)
    all_to_all x6, blocking collectives, swap(): return lax.all_to_all(x, axes, 0, 0, tiled=True)  85.5 us
    ppermute x1, starting transfers between devices, shards(): theirs = lax.ppermute(theirs, 'c', [(0, 1), (1, 0)])  8.79 us
    pallas_call x1, Pallas kernels, gram_rows(): pl.pallas_call(gram_kernel, out_shape=(out, out), in_specs=[pl.BlockSpec(...  3.12 us
    pallas_call x6, Pallas kernels, call(): pl.pallas_call(kernel, grid=(1,), out_shape=out[0] if single else out, in...  2.28 us
  transfers between devices with their start and end apart: 1, of which 1 were waited for; matrix products, arithmetic and copies ran while one was open for 0% of the time, Pallas kernels for 0%

profile of v6, /device:TPU:1, one launch (start us, length us, event | category | flops | bytes accessed | tf_op | source)
XLA Modules:
  0.0 102.2 jit_solution(16988682703279362890)
XLA Ops:
  0.0 0.0 copy-start.2
  0.0 0.9 copy-done.2
  0.9 3.1 %shard_map.46 = (f32[8,4,32,128]{3,2,1,0:T(8,128)S(1)}, f32[8,4,32,128]{3,2,1,0:T(8,128)S(1)}) custom-call(f32[64,512]{1,0:T(8,128)S(1)} %copy-done.2, f32[3,256,512]{2,1,0:T(8,128)} %right_hbm.1, f32[3,256,512]{2,1,0:T(8,128)} %left_ref.1), custom_call_target="tpu_custom_call" | custom-call | tf_op jit(solution)/shard_map/pallas_call | solution.py:106
  4.0 8.8 %collective-permute-start = (f32[8,4,32,128]{3,2,1,0:T(8,128)S(1)}, f32[8,4,32,128]{3,2,1,0:T(8,128)S(1)}, u32[]{:S(2)}, u32[]{:S(2)}) collective-permute-start(f32[8,4,32,128]{3,2,1,0:T(8,128)S(1)} %get-tuple-element.12), channel_id=1, source_target_pairs={{0,1},{1,0},{2,3},{3,2},{4,5},{5,4},{6,7},{7,6},{8,9},{9,8},{10,11... | collective-permute-start | bytes 1572872 | tf_op jit(solution)/shard_map/ppermute | solution.py:228
  12.8 1.5 %collective-permute-done.b_ref = f32[8,4,32,128]{3,2,1,0:T(8,128)S(1)} collective-permute-done((f32[8,4,32,128]{3,2,1,0:T(8,128)S(1)}, f32[8,4,32,128]{3,2,1,0:T(8,128)S(1)}, u32[]{:S(2)}, u32[]{:S(2)}) %collective-permute-start) | collective-permute-done | bytes 524320 | tf_op jit(solution)/shard_map/ppermute | solution.py:228
  14.3 0.1 shard_map.47
  14.4 0.0 copy-start
  14.4 24.0 %all_to_all.30.in_ref = f32[32,32,128]{2,1,0:T(8,128)S(1)} all-to-all(f32[32,32,128]{2,1,0:T(8,128)S(1)} %bitcast.5), channel_id=1, replica_groups=mesh['y2'=2,'y1'=2,'y0'=2,'z'=8,'x'=4,'c'=2] {'z','x'}, dimensions={0} | all-to-all | bytes 1048576 | tf_op jit(solution)/shard_map/all_to_all | solution.py:217
  38.5 11.7 %all_to_all.31.blocks_ref = f32[8,32,128]{2,1,0:T(8,128)S(1)} all-to-all(f32[8,32,128]{2,1,0:T(8,128)S(1)} %shard_map.48), channel_id=1, replica_groups=mesh['y2'=2,'y1'=2,'y0'=2,'z'=8,'x'=4,'c'=2] {'z'}, dimensions={0} | all-to-all | bytes 262144 | tf_op jit(solution)/shard_map/all_to_all | solution.py:217
  50.2 12.5 %all_to_all.32 = f32[16,16,128]{2,1,0:T(8,128)S(1)} all-to-all(f32[16,16,128]{2,1,0:T(8,128)S(1)} %broadcast_in_dim.3), channel_id=1, replica_groups=mesh['y2'=2,'y1'=2,'y0'=2,'z'=8,'x'=4,'c'=2] {'y0','c','x'}, dimensions={0} | all-to-all | bytes 262144 | tf_op jit(solution)/shard_map/all_to_all | solution.py:217
  62.7 0.0 copy-done
  62.7 0.5 shard_map.49
  63.2 0.0 copy-start.1
  63.2 16.5 %all_to_all.33 = f32[32,16,128]{2,1,0:T(8,128)S(1)} all-to-all(f32[32,16,128]{2,1,0:T(8,128)S(1)} %get-tuple-element.13), channel_id=1, replica_groups=mesh['y2'=2,'y1'=2,'y0'=2,'z'=8,'x'=4,'c'=2] {'y1','y0','c','x'}, dimensions={0} | all-to-all | bytes 524288 | tf_op jit(solution)/shard_map/all_to_all | solution.py:217
  79.8 0.4 shard_map.50
  80.2 11.2 %all_to_all.34.got_ref = f32[8,16,128]{2,1,0:T(8,128)S(1)} all-to-all(f32[8,16,128]{2,1,0:T(8,128)S(1)} %get-tuple-element.15), channel_id=1, replica_groups=mesh['y2'=2,'y1'=2,'y0'=2,'z'=8,'x'=4,'c'=2] {'y2','y1','y0'}, dimensions={0} | all-to-all | bytes 131072 | tf_op jit(solution)/shard_map/all_to_all | solution.py:217
  91.4 9.5 %all_to_all.35.got_ref = f32[8,2,16,128]{3,2,1,0:T(8,128)S(1)} all-to-all(f32[8,2,16,128]{3,2,1,0:T(8,128)S(1)} %shard_map.51), channel_id=1, replica_groups=mesh['y2'=2,'y1'=2,'y0'=2,'z'=8,'x'=4,'c'=2] {'c','x'}, dimensions={0} | all-to-all | bytes 262144 | tf_op jit(solution)/shard_map/all_to_all | solution.py:217
  100.9 0.0 copy-done.1
  101.0 1.2 %shard_map.52 = f32[64,512]{1,0:T(8,128)} custom-call(f32[8,2,16,128]{3,2,1,0:T(8,128)S(1)} %all_to_all.35.got_ref, f32[1,3,512,256]{3,2,1,0:T(8,128)S(1)} %copy-done, f32[64,256]{1,0:T(8,128)S(1)} %get-tuple-element.14.coeff0_ref, f32[64,256]{1,0:T(8,128)S(1)} %get-tuple-element.16.coeff1_ref, f32[64,512]{1,0:T(8,128)S(1)} %copy-done.2, ...), custom_call_target="tpu_custom_call" | custom-call | tf_op jit(solution)/shard_map/pallas_call | solution.py:206
  (4 shorter events, 0.1 us)
Async XLA Ops:
  0.0 0.9 copy-start.2
  4.0 10.3 %collective-permute-start = (f32[8,4,32,128]{3,2,1,0:T(8,128)S(1)}, f32[8,4,32,128]{3,2,1,0:T(8,128)S(1)}, u32[]{:S(2)}, u32[]{:S(2)}) collective-permute-start(f32[8,4,32,128]{3,2,1,0:T(8,128)S(1)} %get-tuple-element.12), channel_id=1, source_target_pairs={{0,1},{1,0},{2,3},{3,2},{4,5},{5,4},{6,7},{7,6},{8,9},{9,8},{10,11... | collective-permute-start | bytes 1572872 | tf_op jit(solution)/shard_map/ppermute | solution.py:228
  14.4 48.3 %copy-start = (f32[1,3,512,256]{3,2,1,0:T(8,128)S(1)}, f32[1,3,512,256]{3,2,1,0:T(8,128)}, u32[]{:S(2)}) copy-start(f32[1,3,512,256]{3,2,1,0:T(8,128)} %core_ref.5) | copy-start | bytes 4718596
  63.2 37.7 %copy-start.1 = (f32[3,256,512]{2,1,0:T(8,128)S(1)}, f32[3,256,512]{2,1,0:T(8,128)}, u32[]{:S(2)}) copy-start(f32[3,256,512]{2,1,0:T(8,128)} %left_ref.1) | copy-start | bytes 4718596

commit v7 on v6

--- a/solution.py
+++ b/solution.py
@@ -38,60 +38,34 @@
     return product_t(halves(a), halves(b))
 
 
-def gram_kernel(field_hbm, right_hbm, left_hbm, theirs_ref, mine_ref, field, right, left, sems):
-    first_core = lax.axis_index("c") == 0
-    depth, rank, _ = right.shape
-    rows = rank // 4
-    peers = mine_ref.shape[1]
-    copies = []
-
-    def fetch(src, dst):
-        copy = pltpu.make_async_copy(src, dst, sems.at[len(copies)])
-        copy.start()
-        copies.append(copy)
-
-    fetch(left_hbm.at[0], left.at[0])
-    fetch(right_hbm.at[1], right.at[1])
-    fetch(right_hbm.at[2], right.at[2])
-    fetch(left_hbm.at[1], left.at[1])
-    fetch(field_hbm, field)
-    fetch(right_hbm.at[0], right.at[0])
-
-    def arrived(group):
-        for copy in group:
-            copy.wait()
+def gram_blocks(out_ref, right, left, field, first_group, second_group):
+    depth, _, rows, points = right.shape
+    peers = out_ref.shape[1]
 
     def basis(k):
-        return halves(right[k])
-
-    def pieces(value, s, h):
-        first = 2 * rows * h + HALF * s
-        zero, one = value[first : first + HALF], value[first + rows : first + rows + HALF]
-        return jnp.where(first_core, zero, one), jnp.where(first_core, one, zero)
+        return halves(right[k].reshape(2 * rows, points))
 
     def put(block, value):
         for s in range(peers):
             for h in range(2):
-                for out_ref, piece in zip((mine_ref, theirs_ref), pieces(value, s, h)):
-                    out_ref[block, s, HALF * h : HALF * (h + 1), :] = piece[:, :LANES]
-                    out_ref[block + 1, s, HALF * h : HALF * (h + 1), :] = piece[:, LANES:]
+                piece = value[rows * h + HALF * s : rows * h + HALF * (s + 1)]
+                out_ref[block, s, HALF * h : HALF * (h + 1), :] = piece[:, :LANES]
+                out_ref[block + 1, s, HALF * h : HALF * (h + 1), :] = piece[:, LANES:]
 
     def put_packed(k, value):
         for s in range(peers):
-            both = zip(pieces(value, s, 0), pieces(value, s, 1))
-            for out_ref, piece in zip((mine_ref, theirs_ref), both):
-                out_ref[k // 2, s, HALF * (k % 2) : HALF * (k % 2 + 1), :] = jnp.concatenate(piece, axis=1)
-
-    for out_ref in (mine_ref, theirs_ref):
-        for s in range(peers):
-            out_ref[1, s, HALF:, :] = jnp.zeros((HALF, LANES), jnp.float32)
-    arrived(copies[:3])
-    left_0 = halves(left[0])
-    right_1 = basis(1)
+            pair = [value[rows * h + HALF * s : rows * h + HALF * (s + 1)] for h in range(2)]
+            out_ref[k // 2, s, HALF * (k % 2) : HALF * (k % 2 + 1), :] = jnp.concatenate(pair, axis=1)
+
+    for s in range(peers):
+        out_ref[1, s, HALF:, :] = jnp.zeros((HALF, LANES), jnp.float32)
+    for copy in first_group:
+        copy.wait()
+    left_0, right_1, right_2 = halves(left[0]), basis(1), basis(2)
     put(2, product_t(right_1, left_0))
-    right_2 = basis(2)
     put(4, product_t(right_2, left_0))
-    arrived(copies[3:])
+    for copy in second_group:
+        copy.wait()
     put(6, product_t(right_2, halves(left[1])))
     rhs = halves(field[...])
     put_packed(1, product_t(right_1, rhs))
@@ -99,22 +73,53 @@
     put_packed(0, product_t(basis(0), rhs))
 
 
-def gram_rows(field, right, left):
+def theirs_kernel(field_hbm, right_hbm, left_hbm, theirs_ref, mine, left, field, right, sems):
+    core = lax.axis_index("c")
+    depth, _, rows, _ = right.shape
+    copies = []
+
+    def fetch(src, dst):
+        copy = pltpu.make_async_copy(src, dst, sems.at[len(copies)])
+        copy.start()
+        copies.append(copy)
+
+    def fetch_rows(k, side, dst):
+        for h in range(2):
+            fetch(right_hbm.at[k, pl.ds(rows * (2 * h + side), rows), :], dst.at[k, h])
+
+    fetch(left_hbm.at[0], left.at[0])
+    fetch_rows(1, 1 - core, right)
+    fetch_rows(2, 1 - core, right)
+    early = len(copies)
+    fetch(left_hbm.at[1], left.at[1])
+    fetch(field_hbm, field)
+    fetch_rows(0, 1 - core, right)
+    late = len(copies)
+    for k in range(depth):
+        fetch_rows(k, core, mine)
+    gram_blocks(theirs_ref, right, left, field, copies[:early], copies[early:late])
+    for copy in copies[late:]:
+        copy.wait()
+
+
+def mine_kernel(mine, left, field, out_ref):
+    gram_blocks(out_ref, mine, left, field, (), ())
+
+
+def gram_theirs(field, right, left):
     depth, rank, points = right.shape
     rows = rank // 4
-    out = jax.ShapeDtypeStruct((BLOCKS, rows // HALF, 2 * HALF, LANES), jnp.float32)
+    shapes = ((BLOCKS, rows // HALF, 2 * HALF, LANES), (depth, 2, rows, points), (depth - 1, rank, points), field.shape)
     return pl.pallas_call(
-        gram_kernel,
-        out_shape=(out, out),
+        theirs_kernel,
+        out_shape=tuple(jax.ShapeDtypeStruct(s, jnp.float32) for s in shapes),
         in_specs=[pl.BlockSpec(memory_space=pltpu.HBM)] * 3,
-        out_specs=(pl.BlockSpec(memory_space=pltpu.VMEM),) * 2,
+        out_specs=(pl.BlockSpec(memory_space=pltpu.VMEM),) * 4,
         scratch_shapes=[
-            pltpu.VMEM(field.shape, jnp.float32),
-            pltpu.VMEM((depth, rank, points), jnp.float32),
-            pltpu.VMEM((depth - 1, rank, points), jnp.float32),
-            pltpu.SemaphoreType.DMA((2 * depth,)),
+            pltpu.VMEM((depth, 2, rows, points), jnp.float32),
+            pltpu.SemaphoreType.DMA((4 * depth + depth,)),
         ],
-        compiler_params=pltpu.CompilerParams(vmem_limit_bytes=54000 << 10),
+        compiler_params=pltpu.CompilerParams(vmem_limit_bytes=52000 << 10),
     )(field, right, left)
 
 
@@ -224,8 +229,9 @@
     half = (HALF, LANES)
     rhs, rank = rhs_field.shape[0], right_basis.shape[1]
 
-    theirs, mine = gram_rows(rhs_field, right_basis, left_basis)
+    theirs, *held = gram_theirs(rhs_field, right_basis, left_basis)
     theirs = lax.ppermute(theirs, "c", [(0, 1), (1, 0)])
+    mine = call(mine_kernel, theirs.shape, tuple(held))
     part = call(add_kernel, mine.shape, (mine, theirs))
     part = swap(part.reshape((nz * nx,) + tile), ("z", "x"))
     part = call(sum_spread_kernel, (nz,) + tile, (part,))

time: 103 us -> 102 us (level)
    pallas_call x6 -> x7, Pallas kernels: 2.28 us -> 3.25 us  [call(): pl.pallas_call(kernel, grid=(1,), out_shape=out[0] if single else out, in...]
  transfers between devices with their start and end apart: 1 -> 1, of which waited for: 1 -> 1; matrix products, arithmetic and copies ran while one was open for 0% -> 0% of each run, Pallas kernels for 0% -> 1%
where the time goes in v7:
time: 102 us
  blocking collectives  85.5 us (84%)
  starting transfers between devices  8.78 us (9%)
  Pallas kernels  5.72 us (6%)
    all_to_all x6, blocking collectives, swap(): return lax.all_to_all(x, axes, 0, 0, tiled=True)  85.5 us
    ppermute x1, starting transfers between devices, shards(): theirs = lax.ppermute(theirs, 'c', [(0, 1), (1, 0)])  8.78 us
    pallas_call x7, Pallas kernels, call(): pl.pallas_call(kernel, grid=(1,), out_shape=out[0] if single else out, in...  3.25 us
    pallas_call x1, Pallas kernels, gram_theirs(): pl.pallas_call(theirs_kernel, out_shape=tuple((jax.ShapeDtypeStruct(s, jn...  2.46 us
  transfers between devices with their start and end apart: 1, of which 1 were waited for; matrix products, arithmetic and copies ran while one was open for 0% of the time, Pallas kernels for 1%

profile of v7, /device:TPU:1, one launch (start us, length us, event | category | flops | bytes accessed | tf_op | source)
XLA Modules:
  0.0 101.5 jit_solution(3349008182233891655)
XLA Ops:
  0.0 0.0 copy-start.2
  0.0 0.9 copy-done.2
  0.9 2.5 %shard_map.46 = (f32[8,4,32,128]{3,2,1,0:T(8,128)S(1)}, f32[3,2,64,512]{3,2,1,0:T(8,128)S(1)}, f32[2,256,512]{2,1,0:T(8,128)S(1)}, f32[64,512]{1,0:T(8,128)S(1)}) custom-call(f32[64,512]{1,0:T(8,128)S(1)} %copy-done.2, f32[3,256,512]{2,1,0:T(8,128)} %right_hbm.1, f32[3,256,512]{2,1,0:T(8,128)} %left_ref.1), custom_call_target="tpu_custom_call" | custom-call | tf_op jit(solution)/shard_map/pallas_call | solution.py:113
  3.4 8.8 %collective-permute-start = (f32[8,4,32,128]{3,2,1,0:T(8,128)S(1)}, f32[8,4,32,128]{3,2,1,0:T(8,128)S(1)}, u32[]{:S(2)}, u32[]{:S(2)}) collective-permute-start(f32[8,4,32,128]{3,2,1,0:T(8,128)S(1)} %get-tuple-element.16), channel_id=1, source_target_pairs={{0,1},{1,0},{2,3},{3,2},{4,5},{5,4},{6,7},{7,6},{8,9},{9,8},{10,11... | collective-permute-start | bytes 1572872 | tf_op jit(solution)/shard_map/ppermute | solution.py:233
  12.2 1.0 shard_map.47.a_ref
  13.1 0.5 collective-permute-done.b_ref
  13.7 0.1 shard_map.48
  13.7 0.0 copy-start
  13.8 24.0 %all_to_all.30.in_ref = f32[32,32,128]{2,1,0:T(8,128)S(1)} all-to-all(f32[32,32,128]{2,1,0:T(8,128)S(1)} %bitcast.5), channel_id=1, replica_groups=mesh['y2'=2,'y1'=2,'y0'=2,'z'=8,'x'=4,'c'=2] {'z','x'}, dimensions={0} | all-to-all | bytes 1048576 | tf_op jit(solution)/shard_map/all_to_all | solution.py:222
  37.8 11.7 %all_to_all.31.blocks_ref = f32[8,32,128]{2,1,0:T(8,128)S(1)} all-to-all(f32[8,32,128]{2,1,0:T(8,128)S(1)} %shard_map.49), channel_id=1, replica_groups=mesh['y2'=2,'y1'=2,'y0'=2,'z'=8,'x'=4,'c'=2] {'z'}, dimensions={0} | all-to-all | bytes 262144 | tf_op jit(solution)/shard_map/all_to_all | solution.py:222
  49.5 12.5 %all_to_all.32 = f32[16,16,128]{2,1,0:T(8,128)S(1)} all-to-all(f32[16,16,128]{2,1,0:T(8,128)S(1)} %broadcast_in_dim.3), channel_id=1, replica_groups=mesh['y2'=2,'y1'=2,'y0'=2,'z'=8,'x'=4,'c'=2] {'y0','c','x'}, dimensions={0} | all-to-all | bytes 262144 | tf_op jit(solution)/shard_map/all_to_all | solution.py:222
  62.1 0.0 copy-done
  62.1 0.5 shard_map.50
  62.6 0.0 copy-start.1
  62.6 16.5 %all_to_all.33 = f32[32,16,128]{2,1,0:T(8,128)S(1)} all-to-all(f32[32,16,128]{2,1,0:T(8,128)S(1)} %get-tuple-element.17), channel_id=1, replica_groups=mesh['y2'=2,'y1'=2,'y0'=2,'z'=8,'x'=4,'c'=2] {'y1','y0','c','x'}, dimensions={0} | all-to-all | bytes 524288 | tf_op jit(solution)/shard_map/all_to_all | solution.py:222
  79.1 0.4 shard_map.51
  79.6 11.2 %all_to_all.34.got_ref = f32[8,16,128]{2,1,0:T(8,128)S(1)} all-to-all(f32[8,16,128]{2,1,0:T(8,128)S(1)} %get-tuple-element.19), channel_id=1, replica_groups=mesh['y2'=2,'y1'=2,'y0'=2,'z'=8,'x'=4,'c'=2] {'y2','y1','y0'}, dimensions={0} | all-to-all | bytes 131072 | tf_op jit(solution)/shard_map/all_to_all | solution.py:222
  90.8 9.5 %all_to_all.35.got_ref = f32[8,2,16,128]{3,2,1,0:T(8,128)S(1)} all-to-all(f32[8,2,16,128]{3,2,1,0:T(8,128)S(1)} %shard_map.52), channel_id=1, replica_groups=mesh['y2'=2,'y1'=2,'y0'=2,'z'=8,'x'=4,'c'=2] {'c','x'}, dimensions={0} | all-to-all | bytes 262144 | tf_op jit(solution)/shard_map/all_to_all | solution.py:222
  100.3 0.0 copy-done.1
  100.3 1.2 %shard_map.53 = f32[64,512]{1,0:T(8,128)} custom-call(f32[8,2,16,128]{3,2,1,0:T(8,128)S(1)} %all_to_all.35.got_ref, f32[1,3,512,256]{3,2,1,0:T(8,128)S(1)} %copy-done, f32[64,256]{1,0:T(8,128)S(1)} %get-tuple-element.18.coeff0_ref, f32[64,256]{1,0:T(8,128)S(1)} %get-tuple-element.20.coeff1_ref, f32[64,512]{1,0:T(8,128)S(1)} %copy-done.2, ...), custom_call_target="tpu_custom_call" | custom-call | tf_op jit(solution)/shard_map/pallas_call | solution.py:211
  (4 shorter events, 0.1 us)
Async XLA Ops:
  0.0 0.9 copy-start.2
  3.4 10.3 %collective-permute-start = (f32[8,4,32,128]{3,2,1,0:T(8,128)S(1)}, f32[8,4,32,128]{3,2,1,0:T(8,128)S(1)}, u32[]{:S(2)}, u32[]{:S(2)}) collective-permute-start(f32[8,4,32,128]{3,2,1,0:T(8,128)S(1)} %get-tuple-element.16), channel_id=1, source_target_pairs={{0,1},{1,0},{2,3},{3,2},{4,5},{5,4},{6,7},{7,6},{8,9},{9,8},{10,11... | collective-permute-start | bytes 1572872 | tf_op jit(solution)/shard_map/ppermute | solution.py:233
  13.7 48.3 %copy-start = (f32[1,3,512,256]{3,2,1,0:T(8,128)S(1)}, f32[1,3,512,256]{3,2,1,0:T(8,128)}, u32[]{:S(2)}) copy-start(f32[1,3,512,256]{3,2,1,0:T(8,128)} %core_ref.5) | copy-start | bytes 4718596
  62.6 37.7 %copy-start.1 = (f32[3,256,512]{2,1,0:T(8,128)S(1)}, f32[3,256,512]{2,1,0:T(8,128)}, u32[]{:S(2)}) copy-start(f32[3,256,512]{2,1,0:T(8,128)} %left_ref.1) | copy-start | bytes 4718596

commit v8 on v7

--- a/solution.py
+++ b/solution.py
@@ -38,7 +38,7 @@
     return product_t(halves(a), halves(b))
 
 
-def gram_blocks(out_ref, right, left, field, first_group, second_group):
+def gram_kernel(right, left, field, out_ref):
     depth, _, rows, points = right.shape
     peers = out_ref.shape[1]
 
@@ -59,13 +59,9 @@
 
     for s in range(peers):
         out_ref[1, s, HALF:, :] = jnp.zeros((HALF, LANES), jnp.float32)
-    for copy in first_group:
-        copy.wait()
     left_0, right_1, right_2 = halves(left[0]), basis(1), basis(2)
     put(2, product_t(right_1, left_0))
     put(4, product_t(right_2, left_0))
-    for copy in second_group:
-        copy.wait()
     put(6, product_t(right_2, halves(left[1])))
     rhs = halves(field[...])
     put_packed(1, product_t(right_1, rhs))
@@ -73,9 +69,9 @@
     put_packed(0, product_t(basis(0), rhs))
 
 
-def theirs_kernel(field_hbm, right_hbm, left_hbm, theirs_ref, mine, left, field, right, sems):
+def fetch_kernel(right_hbm, left_hbm, theirs, mine, left, sems):
     core = lax.axis_index("c")
-    depth, _, rows, _ = right.shape
+    depth, _, rows, _ = mine.shape
     copies = []
 
     def fetch(src, dst):
@@ -83,44 +79,27 @@
         copy.start()
         copies.append(copy)
 
-    def fetch_rows(k, side, dst):
-        for h in range(2):
-            fetch(right_hbm.at[k, pl.ds(rows * (2 * h + side), rows), :], dst.at[k, h])
-
-    fetch(left_hbm.at[0], left.at[0])
-    fetch_rows(1, 1 - core, right)
-    fetch_rows(2, 1 - core, right)
-    early = len(copies)
-    fetch(left_hbm.at[1], left.at[1])
-    fetch(field_hbm, field)
-    fetch_rows(0, 1 - core, right)
-    late = len(copies)
+    for j in range(left.shape[0]):
+        fetch(left_hbm.at[j], left.at[j])
     for k in range(depth):
-        fetch_rows(k, core, mine)
-    gram_blocks(theirs_ref, right, left, field, copies[:early], copies[early:late])
-    for copy in copies[late:]:
+        for side, dst in ((1 - core, theirs), (core, mine)):
+            for h in range(2):
+                fetch(right_hbm.at[k, pl.ds(rows * (2 * h + side), rows), :], dst.at[k, h])
+    for copy in copies:
         copy.wait()
 
 
-def mine_kernel(mine, left, field, out_ref):
-    gram_blocks(out_ref, mine, left, field, (), ())
-
-
-def gram_theirs(field, right, left):
+def fetch_bases(right, left):
     depth, rank, points = right.shape
-    rows = rank // 4
-    shapes = ((BLOCKS, rows // HALF, 2 * HALF, LANES), (depth, 2, rows, points), (depth - 1, rank, points), field.shape)
+    rows = jax.ShapeDtypeStruct((depth, 2, rank // 4, points), jnp.float32)
     return pl.pallas_call(
-        theirs_kernel,
-        out_shape=tuple(jax.ShapeDtypeStruct(s, jnp.float32) for s in shapes),
-        in_specs=[pl.BlockSpec(memory_space=pltpu.HBM)] * 3,
-        out_specs=(pl.BlockSpec(memory_space=pltpu.VMEM),) * 4,
-        scratch_shapes=[
-            pltpu.VMEM((depth, 2, rows, points), jnp.float32),
-            pltpu.SemaphoreType.DMA((4 * depth + depth,)),
-        ],
+        fetch_kernel,
+        out_shape=(rows, rows, jax.ShapeDtypeStruct((depth - 1, rank, points), jnp.float32)),
+        in_specs=[pl.BlockSpec(memory_space=pltpu.HBM)] * 2,
+        out_specs=(pl.BlockSpec(memory_space=pltpu.VMEM),) * 3,
+        scratch_shapes=[pltpu.SemaphoreType.DMA((4 * depth + depth - 1,))],
         compiler_params=pltpu.CompilerParams(vmem_limit_bytes=52000 << 10),
-    )(field, right, left)
+    )(right, left)
 
 
 def add_kernel(a_ref, b_ref, out_ref):
@@ -229,9 +208,11 @@
     half = (HALF, LANES)
     rhs, rank = rhs_field.shape[0], right_basis.shape[1]
 
-    theirs, *held = gram_theirs(rhs_field, right_basis, left_basis)
+    their_rows, my_rows, left = fetch_bases(right_basis, left_basis)
+    gram = (BLOCKS, nx, 2 * HALF, LANES)
+    theirs = call(gram_kernel, gram, (their_rows, left, rhs_field))
     theirs = lax.ppermute(theirs, "c", [(0, 1), (1, 0)])
-    mine = call(mine_kernel, theirs.shape, tuple(held))
+    mine = call(gram_kernel, gram, (my_rows, left, rhs_field))
     part = call(add_kernel, mine.shape, (mine, theirs))
     part = swap(part.reshape((nz * nx,) + tile), ("z", "x"))
     part = call(sum_spread_kernel, (nz,) + tile, (part,))

time: 102 us -> 101 us (level)
    pallas_call x7 -> x8, Pallas kernels: 3.25 us -> 4.25 us  [call(): pl.pallas_call(kernel, grid=(1,), out_shape=out[0] if single else out, in...]
where the time goes in v8:
time: 101 us
  blocking collectives  85.5 us (85%)
  starting transfers between devices  8.78 us (9%)
  Pallas kernels  6.06 us (6%)
    all_to_all x6, blocking collectives, swap(): return lax.all_to_all(x, axes, 0, 0, tiled=True)  85.5 us
    ppermute x1, starting transfers between devices, shards(): theirs = lax.ppermute(theirs, 'c', [(0, 1), (1, 0)])  8.78 us
    pallas_call x8, Pallas kernels, call(): pl.pallas_call(kernel, grid=(1,), out_shape=out[0] if single else out, in...  4.25 us
  transfers between devices with their start and end apart: 1, of which 1 were waited for; matrix products, arithmetic and copies ran while one was open for 0% of the time, Pallas kernels for 1%

profile of v8, /device:TPU:1, one launch (start us, length us, event | category | flops | bytes accessed | tf_op | source)
XLA Modules:
  0.0 101.0 jit_solution(11243276209327869617)
XLA Ops:
  0.0 0.0 copy-start.2
  0.0 1.8 %shard_map.46 = (f32[3,2,64,512]{3,2,1,0:T(8,128)S(1)}, f32[3,2,64,512]{3,2,1,0:T(8,128)S(1)}, f32[2,256,512]{2,1,0:T(8,128)S(1)}) custom-call(f32[3,256,512]{2,1,0:T(8,128)} %right_hbm.1, f32[3,256,512]{2,1,0:T(8,128)} %left_ref.1), custom_call_target="tpu_custom_call" | custom-call | tf_op jit(solution)/shard_map/pallas_call | solution.py:95
  1.8 0.0 copy-done.2
  1.8 1.0 shard_map.48
  2.8 8.8 %collective-permute-start = (f32[8,4,32,128]{3,2,1,0:T(8,128)S(1)}, f32[8,4,32,128]{3,2,1,0:T(8,128)S(1)}, u32[]{:S(2)}, u32[]{:S(2)}) collective-permute-start(f32[8,4,32,128]{3,2,1,0:T(8,128)S(1)} %shard_map.48), channel_id=1, source_target_pairs={{0,1},{1,0},{2,3},{3,2},{4,5},{5,4},{6,7},{7,6},{8,9},{9,8},{10,11... | collective-permute-start | bytes 1572872 | tf_op jit(solution)/shard_map/ppermute | solution.py:214
  11.6 1.0 shard_map.47.a_ref
  12.6 0.5 collective-permute-done.b_ref
  13.1 0.1 shard_map.49
  13.2 0.0 copy-start
  13.2 24.0 %all_to_all.30.in_ref = f32[32,32,128]{2,1,0:T(8,128)S(1)} all-to-all(f32[32,32,128]{2,1,0:T(8,128)S(1)} %bitcast.5), channel_id=1, replica_groups=mesh['y2'=2,'y1'=2,'y0'=2,'z'=8,'x'=4,'c'=2] {'z','x'}, dimensions={0} | all-to-all | bytes 1048576 | tf_op jit(solution)/shard_map/all_to_all | solution.py:201
  37.3 11.7 %all_to_all.31.blocks_ref = f32[8,32,128]{2,1,0:T(8,128)S(1)} all-to-all(f32[8,32,128]{2,1,0:T(8,128)S(1)} %shard_map.50), channel_id=1, replica_groups=mesh['y2'=2,'y1'=2,'y0'=2,'z'=8,'x'=4,'c'=2] {'z'}, dimensions={0} | all-to-all | bytes 262144 | tf_op jit(solution)/shard_map/all_to_all | solution.py:201
  49.0 12.5 %all_to_all.32 = f32[16,16,128]{2,1,0:T(8,128)S(1)} all-to-all(f32[16,16,128]{2,1,0:T(8,128)S(1)} %broadcast_in_dim.3), channel_id=1, replica_groups=mesh['y2'=2,'y1'=2,'y0'=2,'z'=8,'x'=4,'c'=2] {'y0','c','x'}, dimensions={0} | all-to-all | bytes 262144 | tf_op jit(solution)/shard_map/all_to_all | solution.py:201
  61.5 0.0 copy-done
  61.5 0.5 shard_map.51
  62.0 0.0 copy-start.1
  62.0 16.5 %all_to_all.33 = f32[32,16,128]{2,1,0:T(8,128)S(1)} all-to-all(f32[32,16,128]{2,1,0:T(8,128)S(1)} %get-tuple-element.15), channel_id=1, replica_groups=mesh['y2'=2,'y1'=2,'y0'=2,'z'=8,'x'=4,'c'=2] {'y1','y0','c','x'}, dimensions={0} | all-to-all | bytes 524288 | tf_op jit(solution)/shard_map/all_to_all | solution.py:201
  78.6 0.4 shard_map.52
  79.0 11.2 %all_to_all.34.got_ref = f32[8,16,128]{2,1,0:T(8,128)S(1)} all-to-all(f32[8,16,128]{2,1,0:T(8,128)S(1)} %get-tuple-element.17), channel_id=1, replica_groups=mesh['y2'=2,'y1'=2,'y0'=2,'z'=8,'x'=4,'c'=2] {'y2','y1','y0'}, dimensions={0} | all-to-all | bytes 131072 | tf_op jit(solution)/shard_map/all_to_all | solution.py:201
  90.2 9.5 %all_to_all.35.got_ref = f32[8,2,16,128]{3,2,1,0:T(8,128)S(1)} all-to-all(f32[8,2,16,128]{3,2,1,0:T(8,128)S(1)} %shard_map.53), channel_id=1, replica_groups=mesh['y2'=2,'y1'=2,'y0'=2,'z'=8,'x'=4,'c'=2] {'c','x'}, dimensions={0} | all-to-all | bytes 262144 | tf_op jit(solution)/shard_map/all_to_all | solution.py:201
  99.7 0.0 copy-done.1
  99.7 1.2 %shard_map.54 = f32[64,512]{1,0:T(8,128)} custom-call(f32[8,2,16,128]{3,2,1,0:T(8,128)S(1)} %all_to_all.35.got_ref, f32[1,3,512,256]{3,2,1,0:T(8,128)S(1)} %copy-done, f32[64,256]{1,0:T(8,128)S(1)} %get-tuple-element.16.coeff0_ref, f32[64,256]{1,0:T(8,128)S(1)} %get-tuple-element.18.coeff1_ref, f32[64,512]{1,0:T(8,128)S(1)} %copy-done.2, ...), custom_call_target="tpu_custom_call" | custom-call | tf_op jit(solution)/shard_map/pallas_call | solution.py:190
  (4 shorter events, 0.1 us)
Async XLA Ops:
  0.0 1.8 %copy-start.2 = (f32[64,512]{1,0:T(8,128)S(1)}, f32[64,512]{1,0:T(8,128)}, u32[]{:S(2)}) copy-start(f32[64,512]{1,0:T(8,128)} %field_ref.1) | copy-start | bytes 393220
  2.8 10.3 %collective-permute-start = (f32[8,4,32,128]{3,2,1,0:T(8,128)S(1)}, f32[8,4,32,128]{3,2,1,0:T(8,128)S(1)}, u32[]{:S(2)}, u32[]{:S(2)}) collective-permute-start(f32[8,4,32,128]{3,2,1,0:T(8,128)S(1)} %shard_map.48), channel_id=1, source_target_pairs={{0,1},{1,0},{2,3},{3,2},{4,5},{5,4},{6,7},{7,6},{8,9},{9,8},{10,11... | collective-permute-start | bytes 1572872 | tf_op jit(solution)/shard_map/ppermute | solution.py:214
  13.2 48.3 %copy-start = (f32[1,3,512,256]{3,2,1,0:T(8,128)S(1)}, f32[1,3,512,256]{3,2,1,0:T(8,128)}, u32[]{:S(2)}) copy-start(f32[1,3,512,256]{3,2,1,0:T(8,128)} %core_ref.5) | copy-start | bytes 4718596
  62.0 37.7 %copy-start.1 = (f32[3,256,512]{2,1,0:T(8,128)S(1)}, f32[3,256,512]{2,1,0:T(8,128)}, u32[]{:S(2)}) copy-start(f32[3,256,512]{2,1,0:T(8,128)} %left_ref.1) | copy-start | bytes 4718596

commit v9 on v8

--- a/solution.py
+++ b/solution.py
@@ -71,7 +71,7 @@
 
 def fetch_kernel(right_hbm, left_hbm, theirs, mine, left, sems):
     core = lax.axis_index("c")
-    depth, _, rows, _ = mine.shape
+    depth = mine.shape[0]
     copies = []
 
     def fetch(src, dst):
@@ -83,8 +83,7 @@
         fetch(left_hbm.at[j], left.at[j])
     for k in range(depth):
         for side, dst in ((1 - core, theirs), (core, mine)):
-            for h in range(2):
-                fetch(right_hbm.at[k, pl.ds(rows * (2 * h + side), rows), :], dst.at[k, h])
+            fetch(right_hbm.at[k, :, side], dst.at[k])
     for copy in copies:
         copy.wait()
 
@@ -97,9 +96,9 @@
         out_shape=(rows, rows, jax.ShapeDtypeStruct((depth - 1, rank, points), jnp.float32)),
         in_specs=[pl.BlockSpec(memory_space=pltpu.HBM)] * 2,
         out_specs=(pl.BlockSpec(memory_space=pltpu.VMEM),) * 3,
-        scratch_shapes=[pltpu.SemaphoreType.DMA((4 * depth + depth - 1,))],
+        scratch_shapes=[pltpu.SemaphoreType.DMA((2 * depth + depth - 1,))],
         compiler_params=pltpu.CompilerParams(vmem_limit_bytes=52000 << 10),
-    )(right, left)
+    )(right.reshape(depth, 2, 2, rank // 4, points), left)
 
 
 def add_kernel(a_ref, b_ref, out_ref):

time: 101 us -> 101 us (level)
  no operation moved by 1% of the time
where the time goes in v9:
time: 101 us
  blocking collectives  85.5 us (85%)
  starting transfers between devices  8.77 us (9%)
  Pallas kernels  6.02 us (6%)
    all_to_all x6, blocking collectives, swap(): return lax.all_to_all(x, axes, 0, 0, tiled=True)  85.5 us
    ppermute x1, starting transfers between devices, shards(): theirs = lax.ppermute(theirs, 'c', [(0, 1), (1, 0)])  8.77 us
    pallas_call x8, Pallas kernels, call(): pl.pallas_call(kernel, grid=(1,), out_shape=out[0] if single else out, in...  4.25 us
  transfers between devices with their start and end apart: 1, of which 1 were waited for; matrix products, arithmetic and copies ran while one was open for 0% of the time, Pallas kernels for 1%

profile of v9, /device:TPU:1, one launch (start us, length us, event | category | flops | bytes accessed | tf_op | source)
XLA Modules:
  0.0 100.9 jit_solution(1530108336004350835)
XLA Ops:
  0.0 0.0 copy-start.2
  0.0 1.8 %shard_map.46 = (f32[3,2,64,512]{3,2,1,0:T(8,128)S(1)}, f32[3,2,64,512]{3,2,1,0:T(8,128)S(1)}, f32[2,256,512]{2,1,0:T(8,128)S(1)}) custom-call(f32[3,2,2,64,512]{4,3,2,1,0:T(8,128)} %bitcast.9, f32[3,256,512]{2,1,0:T(8,128)} %left_ref.1), custom_call_target="tpu_custom_call" | custom-call | tf_op jit(solution)/shard_map/pallas_call | solution.py:94
  1.8 0.0 copy-done.2
  1.8 1.0 shard_map.48
  2.8 8.8 %collective-permute-start = (f32[8,4,32,128]{3,2,1,0:T(8,128)S(1)}, f32[8,4,32,128]{3,2,1,0:T(8,128)S(1)}, u32[]{:S(2)}, u32[]{:S(2)}) collective-permute-start(f32[8,4,32,128]{3,2,1,0:T(8,128)S(1)} %shard_map.48), channel_id=1, source_target_pairs={{0,1},{1,0},{2,3},{3,2},{4,5},{5,4},{6,7},{7,6},{8,9},{9,8},{10,11... | collective-permute-start | bytes 1572872 | tf_op jit(solution)/shard_map/ppermute | solution.py:213
  11.6 1.0 shard_map.47.a_ref
  12.5 0.5 collective-permute-done.b_ref
  13.1 0.1 shard_map.49
  13.1 0.0 copy-start
  13.1 24.0 %all_to_all.30.in_ref = f32[32,32,128]{2,1,0:T(8,128)S(1)} all-to-all(f32[32,32,128]{2,1,0:T(8,128)S(1)} %bitcast.6), channel_id=1, replica_groups=mesh['y2'=2,'y1'=2,'y0'=2,'z'=8,'x'=4,'c'=2] {'z','x'}, dimensions={0} | all-to-all | bytes 1048576 | tf_op jit(solution)/shard_map/all_to_all | solution.py:200
  37.2 11.7 %all_to_all.31.blocks_ref = f32[8,32,128]{2,1,0:T(8,128)S(1)} all-to-all(f32[8,32,128]{2,1,0:T(8,128)S(1)} %shard_map.50), channel_id=1, replica_groups=mesh['y2'=2,'y1'=2,'y0'=2,'z'=8,'x'=4,'c'=2] {'z'}, dimensions={0} | all-to-all | bytes 262144 | tf_op jit(solution)/shard_map/all_to_all | solution.py:200
  48.9 12.5 %all_to_all.32 = f32[16,16,128]{2,1,0:T(8,128)S(1)} all-to-all(f32[16,16,128]{2,1,0:T(8,128)S(1)} %broadcast_in_dim.3), channel_id=1, replica_groups=mesh['y2'=2,'y1'=2,'y0'=2,'z'=8,'x'=4,'c'=2] {'y0','c','x'}, dimensions={0} | all-to-all | bytes 262144 | tf_op jit(solution)/shard_map/all_to_all | solution.py:200
  61.5 0.0 copy-done
  61.5 0.5 shard_map.51
  62.0 0.0 copy-start.1
  62.0 16.5 %all_to_all.33 = f32[32,16,128]{2,1,0:T(8,128)S(1)} all-to-all(f32[32,16,128]{2,1,0:T(8,128)S(1)} %get-tuple-element.15), channel_id=1, replica_groups=mesh['y2'=2,'y1'=2,'y0'=2,'z'=8,'x'=4,'c'=2] {'y1','y0','c','x'}, dimensions={0} | all-to-all | bytes 524288 | tf_op jit(solution)/shard_map/all_to_all | solution.py:200
  78.5 0.4 shard_map.52
  79.0 11.2 %all_to_all.34.got_ref = f32[8,16,128]{2,1,0:T(8,128)S(1)} all-to-all(f32[8,16,128]{2,1,0:T(8,128)S(1)} %get-tuple-element.17), channel_id=1, replica_groups=mesh['y2'=2,'y1'=2,'y0'=2,'z'=8,'x'=4,'c'=2] {'y2','y1','y0'}, dimensions={0} | all-to-all | bytes 131072 | tf_op jit(solution)/shard_map/all_to_all | solution.py:200
  90.2 9.5 %all_to_all.35.got_ref = f32[8,2,16,128]{3,2,1,0:T(8,128)S(1)} all-to-all(f32[8,2,16,128]{3,2,1,0:T(8,128)S(1)} %shard_map.53), channel_id=1, replica_groups=mesh['y2'=2,'y1'=2,'y0'=2,'z'=8,'x'=4,'c'=2] {'c','x'}, dimensions={0} | all-to-all | bytes 262144 | tf_op jit(solution)/shard_map/all_to_all | solution.py:200
  99.7 0.0 copy-done.1
  99.7 1.2 %shard_map.54 = f32[64,512]{1,0:T(8,128)} custom-call(f32[8,2,16,128]{3,2,1,0:T(8,128)S(1)} %all_to_all.35.got_ref, f32[1,3,512,256]{3,2,1,0:T(8,128)S(1)} %copy-done, f32[64,256]{1,0:T(8,128)S(1)} %get-tuple-element.16.coeff0_ref, f32[64,256]{1,0:T(8,128)S(1)} %get-tuple-element.18.coeff1_ref, f32[64,512]{1,0:T(8,128)S(1)} %copy-done.2, ...), custom_call_target="tpu_custom_call" | custom-call | tf_op jit(solution)/shard_map/pallas_call | solution.py:189
  (4 shorter events, 0.1 us)
Async XLA Ops:
  0.0 1.8 %copy-start.2 = (f32[64,512]{1,0:T(8,128)S(1)}, f32[64,512]{1,0:T(8,128)}, u32[]{:S(2)}) copy-start(f32[64,512]{1,0:T(8,128)} %field_ref.1) | copy-start | bytes 393220
  2.8 10.3 %collective-permute-start = (f32[8,4,32,128]{3,2,1,0:T(8,128)S(1)}, f32[8,4,32,128]{3,2,1,0:T(8,128)S(1)}, u32[]{:S(2)}, u32[]{:S(2)}) collective-permute-start(f32[8,4,32,128]{3,2,1,0:T(8,128)S(1)} %shard_map.48), channel_id=1, source_target_pairs={{0,1},{1,0},{2,3},{3,2},{4,5},{5,4},{6,7},{7,6},{8,9},{9,8},{10,11... | collective-permute-start | bytes 1572872 | tf_op jit(solution)/shard_map/ppermute | solution.py:213
  13.1 48.3 %copy-start = (f32[1,3,512,256]{3,2,1,0:T(8,128)S(1)}, f32[1,3,512,256]{3,2,1,0:T(8,128)}, u32[]{:S(2)}) copy-start(f32[1,3,512,256]{3,2,1,0:T(8,128)} %core_ref.5) | copy-start | bytes 4718596
  62.0 37.7 %copy-start.1 = (f32[3,256,512]{2,1,0:T(8,128)S(1)}, f32[3,256,512]{2,1,0:T(8,128)}, u32[]{:S(2)}) copy-start(f32[3,256,512]{2,1,0:T(8,128)} %left_ref.1) | copy-start | bytes 4718596

commit v10 on v9

--- a/solution.py
+++ b/solution.py
@@ -165,10 +165,10 @@
 
 
 def level2_kernel(got_ref, core_ref, coeff0_ref, coeff1_ref, field_ref, left_ref, out_ref):
-    change = mul(coeff0_ref[...], left_ref[0]) + mul(coeff1_ref[...], left_ref[1])
     coeff = coefficients([got_ref[:, 0], got_ref[:, 1]], core_ref)
-    change = change + mul(coeff, left_ref[2])
-    out_ref[...] = field_ref[...] - change
+    levels = jnp.concatenate([coeff0_ref[...], coeff1_ref[...], coeff], axis=1)
+    left = left_ref[...].reshape(levels.shape[1], field_ref.shape[1])
+    out_ref[...] = field_ref[...] - mul(levels, left)
 
 
 def whole(x):

time: 101 us -> 101 us (level)
  no operation moved by 1% of the time
where the time goes in v10:
time: 101 us
  blocking collectives  85.5 us (85%)
  starting transfers between devices  8.77 us (9%)
  Pallas kernels  6.09 us (6%)
    all_to_all x6, blocking collectives, swap(): return lax.all_to_all(x, axes, 0, 0, tiled=True)  85.5 us
    ppermute x1, starting transfers between devices, shards(): theirs = lax.ppermute(theirs, 'c', [(0, 1), (1, 0)])  8.77 us
    pallas_call x8, Pallas kernels, call(): pl.pallas_call(kernel, grid=(1,), out_shape=out[0] if single else out, in...  4.33 us
  transfers between devices with their start and end apart: 1, of which 1 were waited for; matrix products, arithmetic and copies ran while one was open for 0% of the time, Pallas kernels for 1%

profile of v10, /device:TPU:1, one launch (start us, length us, event | category | flops | bytes accessed | tf_op | source)
XLA Modules:
  0.0 101.0 jit_solution(15349273105555388302)
XLA Ops:
  0.0 0.0 copy-start.2
  0.0 1.8 %shard_map.46 = (f32[3,2,64,512]{3,2,1,0:T(8,128)S(1)}, f32[3,2,64,512]{3,2,1,0:T(8,128)S(1)}, f32[2,256,512]{2,1,0:T(8,128)S(1)}) custom-call(f32[3,2,2,64,512]{4,3,2,1,0:T(8,128)} %bitcast.9, f32[3,256,512]{2,1,0:T(8,128)} %left_ref.1), custom_call_target="tpu_custom_call" | custom-call | tf_op jit(solution)/shard_map/pallas_call | solution.py:94
  1.8 0.0 copy-done.2
  1.8 1.0 shard_map.48
  2.8 8.8 %collective-permute-start = (f32[8,4,32,128]{3,2,1,0:T(8,128)S(1)}, f32[8,4,32,128]{3,2,1,0:T(8,128)S(1)}, u32[]{:S(2)}, u32[]{:S(2)}) collective-permute-start(f32[8,4,32,128]{3,2,1,0:T(8,128)S(1)} %shard_map.48), channel_id=1, source_target_pairs={{0,1},{1,0},{2,3},{3,2},{4,5},{5,4},{6,7},{7,6},{8,9},{9,8},{10,11... | collective-permute-start | bytes 1572872 | tf_op jit(solution)/shard_map/ppermute | solution.py:213
  11.6 1.0 shard_map.47.a_ref
  12.5 0.5 collective-permute-done.b_ref
  13.1 0.1 shard_map.49
  13.1 0.0 copy-start
  13.1 24.0 %all_to_all.30.in_ref = f32[32,32,128]{2,1,0:T(8,128)S(1)} all-to-all(f32[32,32,128]{2,1,0:T(8,128)S(1)} %bitcast.6), channel_id=1, replica_groups=mesh['y2'=2,'y1'=2,'y0'=2,'z'=8,'x'=4,'c'=2] {'z','x'}, dimensions={0} | all-to-all | bytes 1048576 | tf_op jit(solution)/shard_map/all_to_all | solution.py:200
  37.2 11.7 %all_to_all.31.blocks_ref = f32[8,32,128]{2,1,0:T(8,128)S(1)} all-to-all(f32[8,32,128]{2,1,0:T(8,128)S(1)} %shard_map.50), channel_id=1, replica_groups=mesh['y2'=2,'y1'=2,'y0'=2,'z'=8,'x'=4,'c'=2] {'z'}, dimensions={0} | all-to-all | bytes 262144 | tf_op jit(solution)/shard_map/all_to_all | solution.py:200
  48.9 12.5 %all_to_all.32 = f32[16,16,128]{2,1,0:T(8,128)S(1)} all-to-all(f32[16,16,128]{2,1,0:T(8,128)S(1)} %broadcast_in_dim.3), channel_id=1, replica_groups=mesh['y2'=2,'y1'=2,'y0'=2,'z'=8,'x'=4,'c'=2] {'y0','c','x'}, dimensions={0} | all-to-all | bytes 262144 | tf_op jit(solution)/shard_map/all_to_all | solution.py:200
  61.5 0.0 copy-done
  61.5 0.5 shard_map.51
  62.0 0.0 copy-start.1
  62.0 16.5 %all_to_all.33 = f32[32,16,128]{2,1,0:T(8,128)S(1)} all-to-all(f32[32,16,128]{2,1,0:T(8,128)S(1)} %get-tuple-element.15), channel_id=1, replica_groups=mesh['y2'=2,'y1'=2,'y0'=2,'z'=8,'x'=4,'c'=2] {'y1','y0','c','x'}, dimensions={0} | all-to-all | bytes 524288 | tf_op jit(solution)/shard_map/all_to_all | solution.py:200
  78.5 0.4 shard_map.52
  79.0 11.2 %all_to_all.34.got_ref = f32[8,16,128]{2,1,0:T(8,128)S(1)} all-to-all(f32[8,16,128]{2,1,0:T(8,128)S(1)} %get-tuple-element.17), channel_id=1, replica_groups=mesh['y2'=2,'y1'=2,'y0'=2,'z'=8,'x'=4,'c'=2] {'y2','y1','y0'}, dimensions={0} | all-to-all | bytes 131072 | tf_op jit(solution)/shard_map/all_to_all | solution.py:200
  90.2 9.5 %all_to_all.35.got_ref = f32[8,2,16,128]{3,2,1,0:T(8,128)S(1)} all-to-all(f32[8,2,16,128]{3,2,1,0:T(8,128)S(1)} %shard_map.53), channel_id=1, replica_groups=mesh['y2'=2,'y1'=2,'y0'=2,'z'=8,'x'=4,'c'=2] {'c','x'}, dimensions={0} | all-to-all | bytes 262144 | tf_op jit(solution)/shard_map/all_to_all | solution.py:200
  99.7 0.0 copy-done.1
  99.7 1.3 %shard_map.54 = f32[64,512]{1,0:T(8,128)} custom-call(f32[8,2,16,128]{3,2,1,0:T(8,128)S(1)} %all_to_all.35.got_ref, f32[1,3,512,256]{3,2,1,0:T(8,128)S(1)} %copy-done, f32[64,256]{1,0:T(8,128)S(1)} %get-tuple-element.16.coeff0_ref, f32[64,256]{1,0:T(8,128)S(1)} %get-tuple-element.18.coeff1_ref, f32[64,512]{1,0:T(8,128)S(1)} %copy-done.2, ...), custom_call_target="tpu_custom_call" | custom-call | tf_op jit(solution)/shard_map/pallas_call | solution.py:189
  (4 shorter events, 0.1 us)
Async XLA Ops:
  0.0 1.8 %copy-start.2 = (f32[64,512]{1,0:T(8,128)S(1)}, f32[64,512]{1,0:T(8,128)}, u32[]{:S(2)}) copy-start(f32[64,512]{1,0:T(8,128)} %field_ref.1) | copy-start | bytes 393220
  2.8 10.3 %collective-permute-start = (f32[8,4,32,128]{3,2,1,0:T(8,128)S(1)}, f32[8,4,32,128]{3,2,1,0:T(8,128)S(1)}, u32[]{:S(2)}, u32[]{:S(2)}) collective-permute-start(f32[8,4,32,128]{3,2,1,0:T(8,128)S(1)} %shard_map.48), channel_id=1, source_target_pairs={{0,1},{1,0},{2,3},{3,2},{4,5},{5,4},{6,7},{7,6},{8,9},{9,8},{10,11... | collective-permute-start | bytes 1572872 | tf_op jit(solution)/shard_map/ppermute | solution.py:213
  13.1 48.3 %copy-start = (f32[1,3,512,256]{3,2,1,0:T(8,128)S(1)}, f32[1,3,512,256]{3,2,1,0:T(8,128)}, u32[]{:S(2)}) copy-start(f32[1,3,512,256]{3,2,1,0:T(8,128)} %core_ref.5) | copy-start | bytes 4718596
  62.0 37.7 %copy-start.1 = (f32[3,256,512]{2,1,0:T(8,128)S(1)}, f32[3,256,512]{2,1,0:T(8,128)}, u32[]{:S(2)}) copy-start(f32[3,256,512]{2,1,0:T(8,128)} %left_ref.1) | copy-start | bytes 4718596
